TPU v7x, 256 devices: a whole 4x4x8 slice. The times are simulated.
256 devices in a mesh: series: 8 (over y, core), tm: 32 (over x, z).
Axes of the slice: x: 4, y: 4, z: 8, core: 2. Of those that a mesh axis runs over, the one named last changes fastest.
Arguments:
- series_data: float32 [8, 131072, 128], P('series', 'tm'), may hold values from -600 to 600, as said below
- cotangent: float32 [8, 131072, 128], P('series', 'tm'), may hold values from -40 to 40, as said below
- in_weight: bfloat16 [128, 128], replicated, may hold values from -0.5 to 0.5
- convolution_weight: bfloat16 [2, 2, 128, 256], replicated, may hold values from -0.375 to 0.375
- convolution_bias: float32 [2, 256], replicated, may hold values from -3 to 3
- res_weight: bfloat16 [128, 128], replicated, may hold values from -0.5 to 0.5
- skip_weight: bfloat16 [2, 128, 256], replicated, may hold values from -0.5 to 0.5
- output_weight: bfloat16 [256, 128], replicated, may hold values from -0.375 to 0.375
- norm_gain_vector: float32 [128], replicated, may hold values from 0.5 to 1.5
- norm_offset_vector: float32 [128], replicated, may hold values from -3 to 3
Outputs:
- series_gradient: float32 [8, 131072, 128], P('series', 'tm')
- conv_grad: float32 [2, 2, 128, 256], replicated
- bias_grad: float32 [2, 256], replicated
- res_grad: float32 [128, 128], replicated
- skip_grad: float32 [2, 128, 256], replicated
- out_grad: float32 [256, 128], replicated
- in_grad: float32 [128, 128], replicated
- gain_grad: float32 [128], replicated
- shift_grad: float32 [128], replicated
Inputs may be any that keep to these rules, and one draw needn't show every extreme that they name: `series_data`: readings of the sensor channels of each series. `cotangent`: loss gradients for each channel and step.
All inputs are finite; a program needn't handle non-finite values.
Results may differ from a plain program's by a relative error of at most 0.0084.
The roundings to bfloat16 on the way count: a program that leaves them out, or rounds other values in their place, can miss the bound.
Values may be sent and summed in bfloat16 or wider, within the bound.
A program may use at most 64 MiB of HBM per device.

v0:
```python
import jax
import jax.numpy as jnp
from jax import lax
from jax.sharding import PartitionSpec as P

FIRST_DILATION = 256
SECOND_DILATION = 512


epsilon = 1e-05
gelu_coeff = 0.7978845608
cubic_coeff = 0.044715


def shifted(block, axis, distance):
    devices = range(lax.axis_size(axis))
    route = [(i - distance, i) for i in devices if i - distance in devices]
    return lax.ppermute(block, axis, route)


def gelu_pair(values):
    inner = gelu_coeff * (values + cubic_coeff * values * values * values)
    tangent = jnp.tanh(inner)
    output = 0.5 * values * (1.0 + tangent)
    slope = 0.5 * (1.0 + tangent) + 0.5 * values * (1.0 - tangent * tangent) * gelu_coeff * (
        1.0 + 3.0 * cubic_coeff * values * values
    )
    return (output, slope)


def matrix_product(left, right):
    return jnp.dot(left, right, preferred_element_type=jnp.float32)


def row_contraction(left, right):
    return lax.dot_general(
        left, right, (((0,), (0,)), ((), ())), preferred_element_type=jnp.float32
    )


def transposed_product(left, right):
    return lax.dot_general(
        left, right, (((1,), (1,)), ((), ())), preferred_element_type=jnp.float32
    )


def gate_window_step(extended, weights, bias, span):
    produced = extended.shape[0] - span
    pre_act = (
        matrix_product(extended[:produced], weights[0])
        + matrix_product(extended[span:], weights[1])
        + bias
    )
    half_cols = pre_act.shape[1] // 2
    gated = (jnp.tanh(pre_act[:, :half_cols]) * jax.nn.sigmoid(pre_act[:, half_cols:])).astype(
        jnp.bfloat16
    )
    return (pre_act, gated)


def gate_backward(pre_act, incoming):
    half_cols = pre_act.shape[1] // 2
    tanh_part = jnp.tanh(pre_act[:, :half_cols])
    sigm_part = jax.nn.sigmoid(pre_act[:, half_cols:])
    return jnp.concatenate(
        [
            incoming * sigm_part * (1.0 - tanh_part * tanh_part),
            incoming * tanh_part * sigm_part * (1.0 - sigm_part),
        ],
        axis=1,
    )


def on_device(
    series_data,
    cotangent,
    in_weight,
    convolution_weight,
    convolution_bias,
    res_weight,
    skip_weight,
    output_weight,
    norm_gain_vector,
    norm_offset_vector,
):
    readings = series_data[0]
    loss_gradient = cotangent[0]
    sequence_length = readings.shape[0]
    total_timesteps = sequence_length * lax.axis_size("tm")
    level_mean = lax.psum(jnp.sum(readings, axis=0), "tm") / total_timesteps
    mean_removed = readings - level_mean
    variance = lax.psum(jnp.sum(mean_removed * mean_removed, axis=0), "tm") / total_timesteps
    inverse_deviation = lax.rsqrt(variance + epsilon)
    spread = jnp.sqrt(variance + epsilon)
    normalized_input = mean_removed * inverse_deviation
    normalized_series = (normalized_input * norm_gain_vector + norm_offset_vector).astype(
        jnp.bfloat16
    )
    zeroth_level = matrix_product(normalized_series, in_weight).astype(jnp.bfloat16)
    zeroth_border = shifted(zeroth_level[sequence_length - FIRST_DILATION :], "tm", 1)
    zeroth_padded = jnp.concatenate([zeroth_border, zeroth_level], axis=0)
    first_activation, first_gated = gate_window_step(
        zeroth_padded, convolution_weight[0], convolution_bias[0], FIRST_DILATION
    )
    first_level = (
        zeroth_level.astype(jnp.float32) + matrix_product(first_gated, res_weight)
    ).astype(jnp.bfloat16)
    first_border = shifted(first_level[sequence_length - SECOND_DILATION :], "tm", 1)
    first_padded = jnp.concatenate([first_border, first_level], axis=0)
    second_activation, second_gated = gate_window_step(
        first_padded, convolution_weight[1], convolution_bias[1], SECOND_DILATION
    )
    skip_total = matrix_product(first_gated, skip_weight[0]) + matrix_product(
        second_gated, skip_weight[1]
    )
    skip_value, skip_slope = gelu_pair(skip_total)
    relu_output = skip_value.astype(jnp.bfloat16)
    prediction = matrix_product(relu_output, output_weight)
    scaled = (loss_gradient * spread / norm_gain_vector).astype(jnp.bfloat16)
    local_a = jnp.sum(loss_gradient, axis=0)
    local_second = jnp.sum(
        loss_gradient * (prediction - norm_offset_vector) / norm_gain_vector, axis=0
    )
    output_first, output_second = lax.psum((local_a, local_second), "tm")
    out_grad = row_contraction(relu_output, scaled)
    back_skip = (transposed_product(scaled, output_weight) * skip_slope).astype(jnp.bfloat16)
    skip_grad = jnp.stack(
        [row_contraction(first_gated, back_skip), row_contraction(second_gated, back_skip)]
    )
    pre_two = gate_backward(second_activation, transposed_product(back_skip, skip_weight[1]))
    second_preactivation_second = pre_two.astype(jnp.bfloat16)
    second_convolved = jnp.stack(
        [
            row_contraction(first_padded[:sequence_length], second_preactivation_second),
            row_contraction(first_padded[SECOND_DILATION:], second_preactivation_second),
        ]
    )
    bias_two = jnp.sum(pre_two, axis=0)
    second_leading = shifted(second_preactivation_second[:SECOND_DILATION], "tm", -1)
    second_trailing = jnp.concatenate([second_preactivation_second, second_leading], axis=0)[
        SECOND_DILATION:
    ]
    first_gradient = (
        transposed_product(second_preactivation_second, convolution_weight[1, 1])
        + transposed_product(second_trailing, convolution_weight[1, 0])
    ).astype(jnp.bfloat16)
    res_grad = row_contraction(first_gated, first_gradient)
    pre_one = gate_backward(
        first_activation,
        transposed_product(back_skip, skip_weight[0])
        + transposed_product(first_gradient, res_weight),
    )
    first_preactivation_second = pre_one.astype(jnp.bfloat16)
    first_convolved = jnp.stack(
        [
            row_contraction(zeroth_padded[:sequence_length], first_preactivation_second),
            row_contraction(zeroth_padded[FIRST_DILATION:], first_preactivation_second),
        ]
    )
    bias_one = jnp.sum(pre_one, axis=0)
    first_leading = shifted(first_preactivation_second[:FIRST_DILATION], "tm", -1)
    first_trailing = jnp.concatenate([first_preactivation_second, first_leading], axis=0)[
        FIRST_DILATION:
    ]
    zeroth_gradient = (
        first_gradient.astype(jnp.float32)
        + transposed_product(first_preactivation_second, convolution_weight[0, 1])
        + transposed_product(first_trailing, convolution_weight[0, 0])
    ).astype(jnp.bfloat16)
    in_grad = row_contraction(normalized_series, zeroth_gradient)
    normalized_gradient = transposed_product(zeroth_gradient, in_weight) * norm_gain_vector
    part_a = jnp.sum(normalized_gradient, axis=0)
    second_portion = jnp.sum(normalized_gradient * normalized_input, axis=0)
    first_total, second_total = lax.psum((part_a, second_portion), "tm")
    series_gradient = (
        inverse_deviation
        * (
            normalized_gradient
            - first_total / total_timesteps
            - normalized_input * second_total / total_timesteps
        )
        + output_first / total_timesteps
        + output_second * normalized_input / total_timesteps
    )
    gain_part = second_portion / norm_gain_vector - local_second * spread / norm_gain_vector
    shift_part = part_a / norm_gain_vector - local_a * spread / norm_gain_vector
    summed = lax.psum(
        (
            first_convolved,
            second_convolved,
            bias_one,
            bias_two,
            res_grad,
            skip_grad,
            out_grad,
            in_grad,
            gain_part,
            shift_part,
        ),
        ("series", "tm"),
    )
    (
        conv_lower,
        conv_upper,
        bias_lower,
        bias_upper,
        res_total,
        skip_total_grad,
        out_total,
        in_total,
        gain_total,
        shift_total,
    ) = summed
    conv_grad = jnp.stack([conv_lower, conv_upper])
    bias_grad = jnp.stack([bias_lower, bias_upper])
    return (
        series_gradient[None],
        conv_grad,
        bias_grad,
        res_total,
        skip_total_grad,
        out_total,
        in_total,
        gain_total,
        shift_total,
    )


def solution(mesh):
    placed = (
        P("series", "tm", None),
        P("series", "tm", None),
        P(),
        P(),
        P(),
        P(),
        P(),
        P(),
        P(),
        P(),
    )
    return jax.shard_map(
        on_device,
        mesh=mesh,
        in_specs=placed,
        out_specs=(P("series", "tm", None), P(), P(), P(), P(), P(), P(), P(), P()),
        check_vma=False,
    )
```

profile of v0, /device:TPU:1, one launch (start us, length us, event | category | flops | bytes accessed | tf_op | source)
XLA Modules:
  0.0 554.7 jit_solution(10853442028714480207)
XLA Ops:
  7.2 0.0 copy-start
  7.2 0.0 all-reduce.5.cloned.1.call-start
  7.3 2.3 reduce_sum.72
  9.6 64.3 %psum.112 = f32[128]{0:T(128)S(1)} all-reduce(f32[128]{0:T(128)S(1)} %reduce_sum.72), channel_id=1, replica_groups=mesh['series'=8,'tm'=32] {'tm'}, use_global_device_ids=true, to_apply=%region_1.0 | all-reduce | flops 128 | bytes 1024 | tf_op jit(solution)/shard_map/psum | solution.py:90
  73.9 0.6 multiply_reduce_fusion.1
  74.5 56.2 %psum.113 = f32[128]{0:T(128)S(1)} all-reduce(f32[128]{0:T(128)S(1)} %multiply_reduce_fusion.1), channel_id=1, replica_groups=mesh['series'=8,'tm'=32] {'tm'}, use_global_device_ids=true, to_apply=%region_3.0 | all-reduce | flops 128 | bytes 1024 | tf_op jit(solution)/shard_map/psum | solution.py:92
  130.7 0.5 convolution_convert_fusion
  131.2 0.6 slice.102
  131.8 3.8 collective-permute-start
  135.6 2.7 fusion.43
  138.3 2.1 reduce_sum.76
  140.4 3.0 fusion.1
  143.4 0.8 multiply_convert_fusion.2
  144.3 0.5 fusion.4
  144.8 0.0 copy-start.5
  144.8 0.7 fusion.34
  145.5 1.5 collective-permute-start.1
  147.0 0.7 fusion.40
  147.8 1.0 collective-permute-done.1
  148.8 0.8 fusion
  149.5 0.8 multiply_convert_fusion.1
  150.4 1.7 multiply_convert_fusion
  152.1 3.0 fusion.2
  155.1 0.4 convolution_bitcast_fusion
  155.5 1.8 subtract_multiply_fusion.3
  157.3 1.0 fusion.28
  158.3 1.5 fusion.68
  159.8 0.3 fusion.15
  160.1 0.3 fusion.16
  160.4 0.4 convolution_bitcast_fusion.1
  160.8 0.8 fusion.38
  161.6 0.8 convolution_bitcast_fusion.2
  162.5 1.5 collective-permute-start.2
  164.0 0.8 convolution_bitcast_fusion.3
  164.8 0.7 maximum_bitcast_fusion.1
  165.6 0.7 pad_maximum_fusion.13
  166.3 0.8 fusion.32
  167.0 3.0 collective-permute-done.2
  170.0 0.8 fusion.5
  170.8 1.1 fusion.73
  171.9 1.4 subtract_multiply_fusion.1
  173.3 0.3 fusion.14
  173.5 0.9 convolution_bitcast_fusion.4
  174.4 0.8 convolution_add_fusion.4
  175.2 1.3 collective-permute-start.3
  176.5 1.7 convolution_bitcast_fusion.5
  178.2 0.3 fusion.13
  178.5 0.7 maximum_bitcast_fusion
  179.2 1.7 collective-permute-done.3
  180.9 0.8 fusion.6
  181.7 1.2 fusion.59
  182.9 1.9 fusion.71
  184.8 57.5 %all-reduce.2 = (f32[128]{0:T(128)S(1)}, f32[128]{0:T(128)S(1)}, f32[128]{0:T(128)S(1)}, f32[128]{0:T(128)S(1)}) all-reduce(f32[128]{0:T(128)S(1)} %fusion.28, f32[128]{0:T(128)S(1)} %reduce_sum.76, f32[128]{0:T(128)S(1)} %get-tuple-element.10, f32[128]{0:T(128)S(1)} %get-tuple-element.9), channel_id=1, replica_groups=mesh['series'=8,'tm'=32] {'tm'}, use_global_device_ids=true, to_apply=%region_11.0 | all-reduce | flops 512 | bytes 4096 | tf_op jit(solution)/shard_map/psum | solution.py:124
  242.3 0.0 all-reduce.5.cloned.1.call-update
  242.4 0.0 copy-start.1
  242.4 3.7 add_bitcast_fusion
  246.1 119.8 %all-reduce = (f32[1,256]{1,0:T(1,128)S(1)}, f32[1,256]{1,0:T(1,128)S(1)}, f32[128]{0:T(128)}, f32[128]{0:T(128)}) all-reduce(f32[1,256]{1,0:T(1,128)S(1)} %bitcast.113, f32[1,256]{1,0:T(1,128)S(1)} %bitcast.114, f32[128]{0:T(128)S(1)} %get-tuple-element.32, ...), channel_id=1, replica_groups=mesh['series'=8,'tm'=32] {'series','tm'}, use_global_device_ids=true, to_apply=%region_17.0 | all-reduce | flops 768 | bytes 6144 | tf_op jit(solution)/shard_map/psum | solution.py:187
  365.9 0.6 pad_maximum_fusion.14
  366.5 173.3 %all-reduce.5.cloned.1.call-done = (f32[1,2,128,256]{3,2,1,0:T(8,128)}, f32[1,2,128,256]{3,2,1,0:T(8,128)}, f32[128,128]{1,0:T(8,128)}, f32[2,128,256]{2,1,0:T(8...) async-done(((f32[1,2,128,256]{3,2,1,0:T(8,128)}, f32[1,2,128,256]{3,2,1,0:T(8,128)}, f32[128,128]{1,0:T(8,128)}, f32[2,128,256]{2,1,0:T(8,128)}, f32[256,128]{1,0:T(8,128)}, ...) | async-done | bytes 1048592 | tf_op jit(solution)/shard_map/psum | solution.py:187
  539.8 1.9 pad_maximum_fusion.12
  541.6 1.5 copy.25
  543.1 1.7 copy.26
  544.8 1.6 copy.27
  546.3 1.5 copy.28
  (28 shorter events, 0.1 us)
Async XLA Ops:
  7.2 144.9 %copy-start = (bf16[256,128]{1,0:T(8,128)(2,1)S(1)}, bf16[256,128]{1,0:T(8,128)(2,1)}, u32[]{:S(2)}) copy-start(bf16[256,128]{1,0:T(8,128)(2,1)} %param.17) | copy-start | bytes 196612
  7.2 66.7 %copy-start.2 = (f32[1,4096,128]{2,1,0:T(8,128)S(1)}, f32[1,4096,128]{2,1,0:T(8,128)}, u32[]{:S(2)}) copy-start(f32[1,4096,128]{2,1,0:T(8,128)} %param.10) | copy-start | bytes 6291460
  7.2 123.5 %copy-start.8 = (f32[128]{0:T(128)S(1)}, f32[128]{0:T(128)}, u32[]{:S(2)}) copy-start(f32[128]{0:T(128)} %param.18) | copy-start | bytes 1540
  7.2 123.5 %copy-start.10 = (f32[128]{0:T(128)S(1)}, f32[128]{0:T(128)}, u32[]{:S(2)}) copy-start(f32[128]{0:T(128)} %param.19) | copy-start | bytes 1540
  7.2 123.5 %copy-start.6 = (bf16[128,128]{1,0:T(8,128)(2,1)S(1)}, bf16[128,128]{1,0:T(8,128)(2,1)}, u32[]{:S(2)}) copy-start(bf16[128,128]{1,0:T(8,128)(2,1)} %param.12) | copy-start | bytes 98308
  7.2 532.5 %all-reduce.5.cloned.1.call-start = ((), (), s32[]{:S(2)}) async-start(), calls=%async_computation | async-start | bytes 2097152 | tf_op jit(solution)/shard_map/psum | solution.py:187
  74.5 61.1 %copy-start.4 = (bf16[2,2,128,256]{3,2,1,0:T(8,128)(2,1)S(1)}, bf16[2,2,128,256]{3,2,1,0:T(8,128)(2,1)}, u32[]{:S(2)}) copy-start(bf16[2,2,128,256]{3,2,1,0:T(8,128)(2,1)} %param.13) | copy-start | bytes 786436
  131.8 6.4 %copy-start.9 = (f32[2,256]{1,0:T(2,128)S(1)}, f32[2,256]{1,0:T(2,128)}, u32[]{:S(2)}) copy-start(f32[2,256]{1,0:T(2,128)} %param.14) | copy-start | bytes 6148
  131.8 8.6 %collective-permute-start = (bf16[256,128]{1,0:T(8,128)(2,1)}, bf16[256,128]{1,0:T(8,128)(2,1)}, u32[]{:S(2)}, u32[]{:S(2)}) collective-permute-start(bf16[256,128]{1,0:T(8,128)(2,1)} %slice.102), channel_id=1, source_target_pairs={{0,1},{1,2},{2,3},{3,4},{4,5},{5,6},{6,7},{7,8},{8,9},{9,10},{10,1... | collective-permute-start | bytes 196616 | tf_op jit(solution)/shard_map/ppermute | solution.py:18
  143.4 0.8 copy-start.7
  144.8 2.3 copy-start.5
  145.5 3.2 collective-permute-start.1
  150.4 1.7 copy-start.3
  162.5 7.5 %collective-permute-start.2 = (bf16[512,256]{0,1:T(8,128)(2,1)S(1)}, bf16[512,256]{0,1:T(8,128)(2,1)S(1)}, u32[]{:S(2)}, u32[]{:S(2)}) collective-permute-start(bf16[512,256]{0,1:T(8,128)(2,1)S(1)} %slice.108), channel_id=1, source_target_pairs={{1,0},{2,1},{3,2},{4,3},{5,4},{6,5},{7,6},{8,7},{9,8},{10,9},{11,1... | collective-permute-start | bytes 786440 | tf_op jit(solution)/shard_map/ppermute | solution.py:18
  175.2 5.7 %collective-permute-start.3 = (bf16[256,256]{0,1:T(8,128)(2,1)S(1)}, bf16[256,256]{0,1:T(8,128)(2,1)S(1)}, u32[]{:S(2)}, u32[]{:S(2)}) collective-permute-start(bf16[256,256]{0,1:T(8,128)(2,1)S(1)} %slice.109), channel_id=1, source_target_pairs={{1,0},{2,1},{3,2},{4,3},{5,4},{6,5},{7,6},{8,7},{9,8},{10,9},{11,1... | collective-permute-start | bytes 393224 | tf_op jit(solution)/shard_map/ppermute | solution.py:18
  242.4 305.5 %copy-start.1 = (bf16[256,128]{1,0:T(8,128)(2,1)S(1)}, bf16[256,128]{1,0:T(8,128)(2,1)}, u32[]{:S(2)}) copy-start(bf16[256,128]{1,0:T(8,128)(2,1)} %param.17) | copy-start | bytes 196612
Sparse Core Ops, SparseCore 0:
  242.5 297.2 all-reduce.4
where the time goes:
time: 556 us; the launch traced here: 555 us
  blocking collectives  298 us (54%)
  waiting for transfers between devices  179 us (32%)
  matrix products  32.3 us (6%)
  other arithmetic  16.1 us (3%)
  between operations  14.4 us (3%)
  starting transfers between devices  8.1 us (1%)
  local copies, waits for them, and re-layouts  6.93 us (1%)
    psum x1, waiting for transfers between devices, on_device(): lax.psum((first_convolved, second_convolved, bias_one, bias_two, res_grad...  173 us
    psum x1, blocking collectives, on_device(): lax.psum((first_convolved, second_convolved, bias_one, bias_two, res_grad...  120 us
    psum x1, blocking collectives, on_device(): level_mean = lax.psum(jnp.sum(readings, axis=0), 'tm') / total_timesteps  64.3 us
    psum x1, blocking collectives, on_device(): output_first, output_second = lax.psum((local_a, local_second), 'tm')  57.5 us
    psum x1, blocking collectives, on_device(): lax.psum(jnp.sum(mean_removed * mean_removed, axis=0), 'tm')  56.2 us
    dot_general x9, matrix products, transposed_product(): lax.dot_general(left, right, (((1,), (1,)), ((), ())), preferred_element_...  12 us
    dot_general x9, matrix products, matrix_product(): return jnp.dot(left, right, preferred_element_type=jnp.float32)  11.5 us
  transfers between devices with their start and end apart: 5, of which 4 were waited for; matrix products, arithmetic and copies ran while one was open for 3% of the time, Pallas kernels for 0%

commit v1 on v0

--- a/solution.py
+++ b/solution.py
@@ -1,6 +1,8 @@
 import jax
 import jax.numpy as jnp
 from jax import lax
+from jax.experimental import pallas as pl
+from jax.experimental.pallas import tpu as pltpu
 from jax.sharding import PartitionSpec as P
 
 FIRST_DILATION = 256
@@ -69,6 +71,254 @@
         ],
         axis=1,
     )
+
+
+TM = 32
+SER = 8
+MESH = pl.DeviceIdType.MESH
+
+
+def greet(pairs):
+    barrier = pltpu.get_barrier_semaphore()
+    total = 0
+    for axis, count in pairs:
+        me = lax.axis_index(axis)
+
+        def hello(k, carry, axis=axis, count=count, me=me):
+            pl.semaphore_signal(
+                barrier, inc=1, device_id={axis: lax.rem(me + k, count)}, device_id_type=MESH
+            )
+            return carry
+
+        lax.fori_loop(1, count, hello, 0)
+        total += count - 1
+    pl.semaphore_wait(barrier, total)
+
+
+def exchange_kernel(own_ref, all_ref, send_sem, recv_sem):
+    me = lax.axis_index("tm")
+    greet([("tm", TM)])
+    all_ref[pl.ds(me, 1)] = own_ref[...][None]
+
+    def copy(peer, slot):
+        return pltpu.make_async_remote_copy(
+            src_ref=own_ref,
+            dst_ref=all_ref.at[slot],
+            send_sem=send_sem.at[peer],
+            recv_sem=recv_sem.at[slot],
+            device_id={"tm": peer},
+            device_id_type=MESH,
+        )
+
+    def send(k, carry):
+        copy(lax.rem(me + k, TM), me).start()
+        return carry
+
+    def finish(k, carry):
+        peer = lax.rem(me + k, TM)
+        copy(peer, peer).wait()
+        return carry
+
+    lax.fori_loop(1, TM, send, 0)
+    lax.fori_loop(1, TM, finish, 0)
+
+
+def exchange(own, collective_id):
+    return pl.pallas_call(
+        exchange_kernel,
+        out_shape=jax.ShapeDtypeStruct((TM, 8, 128), jnp.float32),
+        in_specs=[pl.BlockSpec(memory_space=pltpu.VMEM)],
+        out_specs=pl.BlockSpec(memory_space=pltpu.VMEM),
+        scratch_shapes=[pltpu.SemaphoreType.DMA((TM,)), pltpu.SemaphoreType.DMA((TM,))],
+        compiler_params=pltpu.CompilerParams(collective_id=collective_id, has_side_effects=True),
+    )(own)
+
+
+def reduce_kernel(
+    grads_ref,
+    small_ref,
+    out_ref,
+    small_out_ref,
+    recv_one,
+    block,
+    recv_two,
+    small_all,
+    s_one,
+    r_one,
+    s_two,
+    r_two,
+    s_three,
+    r_three,
+    s_four,
+    r_four,
+    s_small,
+    r_small,
+):
+    ser = lax.axis_index("series")
+    tm = lax.axis_index("tm")
+    greet([("series", SER), ("tm", TM)])
+
+    def remote(src, dst, s_sem, r_sem, axis, peer):
+        return pltpu.make_async_remote_copy(
+            src_ref=src,
+            dst_ref=dst,
+            send_sem=s_sem,
+            recv_sem=r_sem,
+            device_id={axis: peer},
+            device_id_type=MESH,
+        )
+
+    def rows(start, size):
+        return pl.ds(pl.multiple_of(start, 8), size)
+
+    def each(lo, hi, body):
+        def run(k, carry):
+            body(k)
+            return carry
+
+        lax.fori_loop(lo, hi, run, 0)
+
+    def one(g, peer, slot):
+        return remote(
+            grads_ref.at[rows(g * 1024 + peer * 128, 128)],
+            recv_one.at[g, slot],
+            s_one.at[g, peer],
+            r_one.at[g, slot],
+            "series",
+            peer,
+        )
+
+    def small(peer, slot):
+        return remote(
+            small_ref, small_all.at[slot], s_small.at[peer], r_small.at[slot], "series", peer
+        )
+
+    def two(g, piece, slot):
+        return remote(
+            block.at[g, rows(piece * 8, 8)],
+            recv_two.at[slot],
+            s_two.at[g, piece],
+            r_two.at[slot],
+            "tm",
+            g * 16 + piece,
+        )
+
+    def three(g, piece, peer):
+        where = out_ref.at[rows(g * 1024 + ser * 128 + piece * 8, 8)]
+        return remote(where, where, s_three.at[peer], r_three.at[g, piece], "tm", peer)
+
+    def four(g, peer, slot):
+        where = out_ref.at[rows(g * 1024 + slot * 128, 128)]
+        return remote(where, where, s_four.at[g, peer], r_four.at[g, slot], "series", peer)
+
+    small_all[pl.ds(ser, 1)] = small_ref[...][None]
+    for g in range(2):
+        each(1, SER, lambda k: one(g, lax.rem(ser + k, SER), ser).start())
+    each(1, SER, lambda k: small(lax.rem(ser + k, SER), ser).start())
+    for g in range(2):
+
+        def take(k):
+            peer = lax.rem(ser + k, SER)
+            one(g, peer, peer).wait()
+
+        each(1, SER, take)
+        total = grads_ref[rows(g * 1024 + ser * 128, 128)]
+        recv_one[g, pl.ds(ser, 1)] = total[None]
+        total = recv_one[g, 0]
+        for s in range(1, SER):
+            total = total + recv_one[g, s]
+        block[g] = total
+
+        def push(piece):
+            @pl.when(g * 16 + piece != tm)
+            def _():
+                two(g, piece, tm).start()
+
+        each(0, 16, push)
+    for g in range(2):
+
+        @pl.when(tm // 16 == g)
+        def _():
+            mine = tm - g * 16
+
+            def pull(k):
+                peer = lax.rem(tm + k, TM)
+                two(g, mine, peer).wait_recv()
+
+            each(1, TM, pull)
+            recv_two[pl.ds(tm, 1)] = block[g, rows(mine * 8, 8)][None]
+            total = recv_two[0]
+            for t in range(1, TM):
+                total = total + recv_two[t]
+            out_ref[rows(g * 1024 + ser * 128 + mine * 8, 8)] = total
+            each(1, TM, lambda k: three(g, mine, lax.rem(tm + k, TM)).start())
+
+    for g in range(2):
+
+        def arrive(piece):
+            @pl.when(g * 16 + piece != tm)
+            def _():
+                two(g, piece, tm).wait_send()
+                three(g, piece, g * 16 + piece).wait_recv()
+
+        each(0, 16, arrive)
+        each(1, SER, lambda k: four(g, lax.rem(ser + k, SER), ser).start())
+    for g in range(2):
+
+        @pl.when(tm // 16 == g)
+        def _():
+            each(1, TM, lambda k: three(g, tm - g * 16, lax.rem(tm + k, TM)).wait_send())
+
+    def last(k):
+        peer = lax.rem(ser + k, SER)
+        small(peer, peer).wait()
+
+    each(1, SER, last)
+    total = small_all[0]
+    for s in range(1, SER):
+        total = total + small_all[s]
+    small_out_ref[...] = total
+    for g in range(2):
+
+        def done(k):
+            peer = lax.rem(ser + k, SER)
+            four(g, peer, ser).wait_send()
+            four(g, peer, peer).wait_recv()
+
+        each(1, SER, done)
+
+
+def reduce_all(grads, small):
+    vmem = pl.BlockSpec(memory_space=pltpu.VMEM)
+    sem = pltpu.SemaphoreType.DMA
+    return pl.pallas_call(
+        reduce_kernel,
+        out_shape=(
+            jax.ShapeDtypeStruct((2048, 128), jnp.float32),
+            jax.ShapeDtypeStruct((8, 128), jnp.float32),
+        ),
+        in_specs=[vmem, vmem],
+        out_specs=(vmem, vmem),
+        scratch_shapes=[
+            pltpu.VMEM((2, SER, 128, 128), jnp.float32),
+            pltpu.VMEM((2, 128, 128), jnp.float32),
+            pltpu.VMEM((TM, 8, 128), jnp.float32),
+            pltpu.VMEM((SER, 8, 128), jnp.float32),
+            sem((2, SER)),
+            sem((2, SER)),
+            sem((2, 16)),
+            sem((TM,)),
+            sem((TM,)),
+            sem((2, 16)),
+            sem((2, SER)),
+            sem((2, SER)),
+            sem((SER,)),
+            sem((SER,)),
+        ],
+        compiler_params=pltpu.CompilerParams(
+            collective_id=2, has_side_effects=True, vmem_limit_bytes=24 * 1024 * 1024
+        ),
+    )(grads, small)
 
 
 def on_device(
@@ -87,9 +337,17 @@
     loss_gradient = cotangent[0]
     sequence_length = readings.shape[0]
     total_timesteps = sequence_length * lax.axis_size("tm")
-    level_mean = lax.psum(jnp.sum(readings, axis=0), "tm") / total_timesteps
+    local_sum = jnp.sum(readings, axis=0)
+    local_mean = local_sum / sequence_length
+    local_centred = jnp.sum(jnp.square(readings - local_mean), axis=0)
+    zero = jnp.zeros((6, 128), jnp.float32)
+    parts = exchange(jnp.concatenate([local_sum[None], local_centred[None], zero]), 0)
+    level_mean = jnp.sum(parts[:, 0], axis=0) / total_timesteps
+    spreads = jnp.square(parts[:, 0] / sequence_length - level_mean)
+    variance = (
+        jnp.sum(parts[:, 1], axis=0) + sequence_length * jnp.sum(spreads, axis=0)
+    ) / total_timesteps
     mean_removed = readings - level_mean
-    variance = lax.psum(jnp.sum(mean_removed * mean_removed, axis=0), "tm") / total_timesteps
     inverse_deviation = lax.rsqrt(variance + epsilon)
     spread = jnp.sqrt(variance + epsilon)
     normalized_input = mean_removed * inverse_deviation
@@ -121,7 +379,6 @@
     local_second = jnp.sum(
         loss_gradient * (prediction - norm_offset_vector) / norm_gain_vector, axis=0
     )
-    output_first, output_second = lax.psum((local_a, local_second), "tm")
     out_grad = row_contraction(relu_output, scaled)
     back_skip = (transposed_product(scaled, output_weight) * skip_slope).astype(jnp.bfloat16)
     skip_grad = jnp.stack(
@@ -171,7 +428,18 @@
     normalized_gradient = transposed_product(zeroth_gradient, in_weight) * norm_gain_vector
     part_a = jnp.sum(normalized_gradient, axis=0)
     second_portion = jnp.sum(normalized_gradient * normalized_input, axis=0)
-    first_total, second_total = lax.psum((part_a, second_portion), "tm")
+    parts = exchange(
+        jnp.concatenate(
+            [
+                jnp.stack([part_a, second_portion, local_a, local_second]),
+                bias_one.reshape(2, 128),
+                bias_two.reshape(2, 128),
+            ]
+        ),
+        1,
+    )
+    parts = jnp.sum(parts, axis=0)
+    first_total, second_total, output_first, output_second = parts[0], parts[1], parts[2], parts[3]
     series_gradient = (
         inverse_deviation
         * (
@@ -182,37 +450,36 @@
         + output_first / total_timesteps
         + output_second * normalized_input / total_timesteps
     )
-    gain_part = second_portion / norm_gain_vector - local_second * spread / norm_gain_vector
-    shift_part = part_a / norm_gain_vector - local_a * spread / norm_gain_vector
-    summed = lax.psum(
-        (
-            first_convolved,
-            second_convolved,
-            bias_one,
-            bias_two,
+    gain_part = second_total / norm_gain_vector - output_second * spread / norm_gain_vector
+    shift_part = first_total / norm_gain_vector - output_first * spread / norm_gain_vector
+    halves = lambda a: jnp.concatenate([a[..., :128], a[..., 128:]], axis=-2).reshape(-1, 128)
+    grads = jnp.concatenate(
+        [
+            halves(second_convolved),
+            halves(skip_grad),
+            halves(first_convolved),
+            out_grad,
             res_grad,
-            skip_grad,
-            out_grad,
             in_grad,
-            gain_part,
-            shift_part,
-        ),
-        ("series", "tm"),
-    )
-    (
-        conv_lower,
-        conv_upper,
-        bias_lower,
-        bias_upper,
-        res_total,
-        skip_total_grad,
-        out_total,
-        in_total,
-        gain_total,
-        shift_total,
-    ) = summed
-    conv_grad = jnp.stack([conv_lower, conv_upper])
-    bias_grad = jnp.stack([bias_lower, bias_upper])
+        ]
+    )
+    small = jnp.concatenate(
+        [gain_part[None], shift_part[None], parts[4:], jnp.zeros((2, 128), jnp.float32)]
+    )
+    reduced, small = reduce_all(grads, small)
+
+    def join(block):
+        block = block.reshape(-1, 2, 128, 128)
+        return jnp.concatenate([block[:, 0], block[:, 1]], axis=-1)
+
+    conv_grad = jnp.stack([join(reduced[1024:1536]), join(reduced[:512])])
+    skip_total_grad = join(reduced[512:1024])
+    out_total = reduced[1536:1792]
+    res_total = reduced[1792:1920]
+    in_total = reduced[1920:]
+    gain_total = small[0]
+    shift_total = small[1]
+    bias_grad = small[2:6].reshape(2, 256)
     return (
         series_gradient[None],
         conv_grad,

time: 556 us -> 153 us (0.28)
  blocking collectives: 298 us -> 0 us
  waiting for transfers between devices: 179 us -> 10.4 us
  Pallas kernels: 0 us -> 80.7 us
  between operations: 14.4 us -> 1.21 us
    psum x4 -> x0, blocking collectives: 298 us -> none  [the longest x1 120 us: on_device(): lax.psum((first_convolved, second_convolved, bias_one, bias_two, res_grad...]
    psum x1 -> x0, waiting for transfers between devices: 173 us -> none  [on_device(): lax.psum((first_convolved, second_convolved, bias_one, bias_two, res_grad...]
    pallas_call x0 -> x3, Pallas kernels: none -> 80.7 us  [the longest x1 47.3 us: reduce_all(): pl.pallas_call(reduce_kernel, out_shape=(jax.ShapeDtypeStruct((2048, 128)...]
  transfers between devices with their start and end apart: 5 -> 4, of which waited for: 4 -> 3; matrix products, arithmetic and copies ran while one was open for 3% -> 5% of each run, Pallas kernels for 0% -> 0%
where the time goes in v1:
time: 153 us
  Pallas kernels  80.7 us (53%)
  matrix products  32.5 us (21%)
  other arithmetic  14.3 us (9%)
  waiting for transfers between devices  10.4 us (7%)
  starting transfers between devices  7.89 us (5%)
  local copies, waits for them, and re-layouts  5.91 us (4%)
    pallas_call x1, Pallas kernels, reduce_all(): pl.pallas_call(reduce_kernel, out_shape=(jax.ShapeDtypeStruct((2048, 128)...  47.3 us
    pallas_call x2, Pallas kernels, exchange(): pl.pallas_call(exchange_kernel, out_shape=jax.ShapeDtypeStruct((TM, 8, 12...  33.5 us
    dot_general x9, matrix products, transposed_product(): lax.dot_general(left, right, (((1,), (1,)), ((), ())), preferred_element_...  12 us
    dot_general x9, matrix products, matrix_product(): return jnp.dot(left, right, preferred_element_type=jnp.float32)  11.4 us
    ppermute x4, waiting for transfers between devices, shifted(): return lax.ppermute(block, axis, route)  10.4 us
    dot_general x9, matrix products, row_contraction(): lax.dot_general(left, right, (((0,), (0,)), ((), ())), preferred_element_...  9.09 us
    ppermute x4, starting transfers between devices, shifted(): return lax.ppermute(block, axis, route)  7.89 us
  transfers between devices with their start and end apart: 4, of which 3 were waited for; matrix products, arithmetic and copies ran while one was open for 5% of the time, Pallas kernels for 0%

profile of v1, /device:TPU:1, one launch (start us, length us, event | category | flops | bytes accessed | tf_op | source)
XLA Modules:
  0.0 152.9 jit_solution(13310387063408767966)
XLA Ops:
  0.7 2.3 %reduce_sum.108 = f32[128]{0:T(128)S(1)} reduce(f32[1,4096,128]{2,1,0:T(8,128)} %param.10, f32[]{:T(128)} %constant.10.clone.1), dimensions={0,1}, to_apply=%region_0.0 | reduce | flops 524160 | bytes 2097668 | tf_op jit(solution)/shard_map/reduce_sum | solution.py:340
  3.0 0.6 fusion.28
  3.6 0.1 pad.38.clone
  3.7 0.7 maximum_maximum_fusion.own_ref
  4.3 16.9 %shard_map.169 = f32[32,8,128]{2,1,0:T(8,128)} custom-call(f32[8,128]{1,0:T(8,128)} %maximum_maximum_fusion.own_ref), custom_call_target="tpu_custom_call" | custom-call | tf_op jit(solution)/shard_map/pallas_call | solution.py:127
  21.3 1.0 slice_reduce_fusion
  22.4 0.5 convolution_convert_fusion
  22.9 0.7 slice.215
  23.6 3.1 %collective-permute-start = (bf16[256,128]{1,0:T(8,128)(2,1)}, bf16[256,128]{1,0:T(8,128)(2,1)}, u32[]{:S(2)}, u32[]{:S(2)}) collective-permute-start(bf16[256,128]{1,0:T(8,128)(2,1)} %slice.215), channel_id=1, source_target_pairs={{0,1},{1,2},{2,3},{3,4},{4,5},{5,6},{6,7},{7,8},{8,9},{9,10},{10,1... | collective-permute-start | bytes 196616 | tf_op jit(solution)/shard_map/ppermute | solution.py:20
  26.6 2.7 %fusion.51 = f32[4096,256]{0,1:T(8,128)} fusion(bf16[4096,128]{1,0:T(8,128)(2,1)S(1)} %convolution_convert_fusion, bf16[2,2,128,256]{3,2,1,0:T(8,128)(2,1)S(1)} %copy-done.8), kind=kOutput, calls=%fused_computation.116 | convolution fusion | flops 268435456 | bytes 5308416 | tf_op jit(solution)/shard_map/dot_general | solution.py:34
  29.3 2.1 %reduce_sum.115 = f32[128]{0:T(128)S(1)} reduce(f32[1,4096,128]{2,1,0:T(8,128)} %param.11, f32[]{:T(128)} %constant.10.clone.1), dimensions={0,1}, to_apply=%region_7.0 | reduce | flops 524160 | bytes 2097668 | tf_op jit(solution)/shard_map/reduce_sum | solution.py:378
  31.4 0.1 pad.11.clone
  31.5 3.0 %fusion.1 = f32[4096,256]{0,1:T(8,128)S(1)} fusion(f32[4096,256]{0,1:T(8,128)} %fusion.51, f32[256]{0:T(256)S(1)} %bitcast.191, bf16[4096,128]{1,0:T(8,128)(2,1)S(1)} %convolution_convert_fusion, bf16[256,128]{1,0:T(8,128)(2,1)} %collective-permute-done, bf16[2,2,128,256]{3,2,1,0:T(8,128)(2,1)S(1)} %copy-done.8), kind=kOutput, calls=%fused_computation.6 | convolution fusion | flops 272629760 | bytes 9569280 | tf_op jit(solution)/shard_map/dot_general | solution.py:34
  34.5 0.8 multiply_convert_fusion.2
  35.4 0.5 fusion.4
  35.9 0.7 fusion.42
  36.6 2.0 %collective-permute-start.1 = (bf16[512,128]{1,0:T(8,128)(2,1)S(1)}, bf16[512,128]{1,0:T(8,128)(2,1)S(1)}, u32[]{:S(2)}, u32[]{:S(2)}) collective-permute-start(bf16[512,128]{1,0:T(8,128)(2,1)S(1)} %slice.218), channel_id=1, source_target_pairs={{0,1},{1,2},{2,3},{3,4},{4,5},{5,6},{6,7},{7,8},{8,9},{9,10},{10,1... | collective-permute-start | bytes 393224 | tf_op jit(solution)/shard_map/ppermute | solution.py:20
  38.7 0.7 fusion.48
  39.4 1.0 collective-permute-done.1
  40.4 0.8 fusion
  41.2 0.8 multiply_convert_fusion.1
  42.0 0.8 convolution_add_fusion
  42.8 0.8 copy-done.7
  43.6 1.8 %fusion.30 = f32[128]{0:T(128)S(1)} fusion(bf16[256,128]{1,0:T(8,128)(2,1)S(1)} %copy-done, f32[1,4096,128]{2,1,0:T(8,128)S(1)} %copy-done.7, f32[128]{0:T(128)S(1)} %copy-done.14, f32[128]{0:T(128)S(1)} %copy-done.12, f32[4096,256]{1,0:T(8,128)S(1)} %convolution_add_fusion), kind=kOutput, calls=%fused_computation.65 | convolution fusion | flops 279969664 | bytes 6358528 | tf_op jit(solution)/shard_map/dot_general | solution.py:34
  45.4 3.0 %fusion.2 = bf16[4096,256]{1,0:T(8,128)(2,1)S(1)} fusion(bf16[256,128]{1,0:T(8,128)(2,1)S(1)} %copy-done, f32[4096,256]{1,0:T(8,128)S(1)} %convolution_add_fusion, f32[1,4096,128]{2,1,0:T(8,128)S(1)} %copy-done.7, f32[128]{0:T(128)S(1)} %copy-done.12, f32[128]{0:T(128)S(1)} %get-tuple-element.17), kind=kOutput, calls=%fused_computation.8 | convolution fusion | flops 289931264 | bytes 8455168 | tf_op jit(solution)/shard_map/dot_general | solution.py:44
  48.4 0.5 convolution_bitcast_fusion.2
  48.9 1.8 %subtract_multiply_fusion.3 = (f32[4096,128]{0,1:T(8,128)S(1)}, f32[4096,128]{0,1:T(8,128)S(1)}) fusion(f32[4096,256]{0,1:T(8,128)S(1)} %fusion, bf16[4096,256]{1,0:T(8,128)(2,1)S(1)} %fusion.2, bf16[2,128,256]{2,1,0:T(8,128)(2,1)S(1)} %copy-done.9), kind=kOutput, calls=%fused_computation.61 | convolution fusion | flops 274202624 | bytes 10551296 | tf_op jit(solution)/shard_map/dot_general | solution.py:44
  50.6 0.3 fusion.15
  50.9 0.3 fusion.16
  51.2 0.4 convolution_bitcast_fusion.3
  51.7 0.8 fusion.46
  52.5 0.8 convolution_bitcast_fusion.4
  53.4 0.8 convolution_bitcast_fusion.5
  54.3 1.5 collective-permute-start.2
  55.8 0.8 fusion.40
  56.6 5.2 %collective-permute-done.2 = bf16[512,256]{0,1:T(8,128)(2,1)S(1)} collective-permute-done((bf16[512,256]{0,1:T(8,128)(2,1)S(1)}, bf16[512,256]{0,1:T(8,128)(2,1)S(1)}, u32[]{:S(2)}, u32[]{:S(2)}) %collective-permute-start.2) | collective-permute-done | bytes 262176 | tf_op jit(solution)/shard_map/ppermute | solution.py:20
  61.8 0.8 fusion.5
  62.6 1.4 subtract_multiply_fusion.1
  64.0 0.3 fusion.14
  64.3 0.9 copy-done.4
  65.2 0.8 convolution_bitcast_fusion
  66.1 0.8 convolution_add_fusion.4
  66.9 1.7 %convolution_bitcast_fusion.1 = f32[1,128,256]{2,1,0:T(8,128)S(1)} fusion(bf16[4096,256]{0,1:T(8,128)(2,1)S(1)} %fusion.14, bf16[4096,128]{1,0:T(8,128)(2,1)S(1)} %copy-done.4, bf16[256,128]{1,0:T(8,128)(2,1)} %collective-permute-done), kind=kOutput, calls=%fused_computation.68 | convolution fusion | flops 270532608 | bytes 3342336 | tf_op jit(solution)/shard_map/dot_general | solution.py:38
  68.6 1.8 %convolution_dynamic-update-slice_fusion = f32[2048,128]{1,0:T(8,128)S(1)} fusion(f32[2048,128]{1,0:T(8,128)S(1)} %constant_dynamic-update-slice_fusion, f32[1,4096,128]{2,1,0:T(8,128)S(1)} %copy-done.7, f32[128]{0:T(128)S(1)} %copy-done.12, f32[128]{0:T(128)S(1)} %get-tuple-element.17, f32[4096,256]{1,0:T(8,128)S(1)} %convolution_add_fusion), kind=kOutput, calls=%fused_computation.66 | convolution fusion | flops 279445504 | bytes 6423552 | tf_op jit(solution)/shard_map/dot_general | solution.py:38
  70.4 1.3 collective-permute-start.3
  71.7 0.4 convolution_dynamic-update-slice_fusion.2
  72.2 0.3 fusion.13
  72.4 4.2 %collective-permute-done.3 = bf16[256,256]{0,1:T(8,128)(2,1)S(1)} collective-permute-done((bf16[256,256]{0,1:T(8,128)(2,1)S(1)}, bf16[256,256]{0,1:T(8,128)(2,1)S(1)}, u32[]{:S(2)}, u32[]{:S(2)}) %collective-permute-start.3) | collective-permute-done | bytes 131104 | tf_op jit(solution)/shard_map/ppermute | solution.py:20
  76.7 0.8 fusion.6
  77.5 2.0 %multiply_reduce_fusion = (f32[128]{0:T(128)S(1)}, f32[128]{0:T(128)S(1)}, f32[4096,128]{1,0:T(8,128)}) fusion(f32[1,4096,128]{2,1,0:T(8,128)S(1)} %copy-done.2, f32[128]{0:T(128)S(1)} %broadcast_multiply_fusion, f32[128]{0:T(128)S(1)} %rsqrt.7, f32[128]{0:T(128)S(1)} %copy-done.12, bf16[4096,128]{1,0:T(8,128)(2,1)S(1)} %fusion.6, ...), kind=kOutput, calls=%fused_computation.57 | convolution fusion | flops 137363200 | bytes 5278208 | tf_op jit(solution)/shard_map/dot_general | solution.py:44
  79.4 0.6 concatenate.55.own_ref
  80.0 16.6 %shard_map.170 = f32[32,8,128]{2,1,0:T(8,128)} custom-call(f32[8,128]{1,0:T(8,128)} %concatenate.55.own_ref), custom_call_target="tpu_custom_call" | custom-call | tf_op jit(solution)/shard_map/pallas_call | solution.py:127
  96.6 0.9 reduce_sum.119
  97.6 1.8 %convolution_dynamic-update-slice_fusion.1.grads_ref = f32[2048,128]{1,0:T(8,128)S(1)} fusion(f32[2048,128]{1,0:T(8,128)S(1)} %convolution_dynamic-update-slice_fusion.2, bf16[4096,128]{1,0:T(8,128)(2,1)} %copy-done.6, f32[1,4096,128]{2,1,0:T(8,128)S(1)} %copy-done.2, f32[128]{0:T(128)S(1)} %copy-done.14, f32[128]{0:T(128)S(1)} %broadcast_multiply_fusion, ...), kind=kOutput, calls=%fused_computation.73 | convolution fusion | flops 136839168 | bytes 3213312 | tf_op jit(solution)/shard_map/dot_general | solution.py:38
  99.4 0.1 maximum_maximum_fusion.1.small_ref
  99.4 47.3 %shard_map.171 = (f32[2048,128]{1,0:T(8,128)S(1)}, f32[8,128]{1,0:T(8,128)S(1)}) custom-call(f32[2048,128]{1,0:T(8,128)S(1)} %convolution_dynamic-update-slice_fusion.1.grads_ref, f32[8,128]{1,0:T(8,128)S(1)} %maximum_maximum_fusion.1.small_ref), custom_call_target="tpu_custom_call" | custom-call | tf_op jit(solution)/shard_map/pallas_call | solution.py:294
  146.7 0.5 slice_bitcast_fusion.6
  147.2 0.7 slice.211
  147.9 0.7 fusion.79
  148.5 0.1 fusion.80
  148.6 0.6 reshape.84
  149.3 0.7 pad_maximum_fusion.16
  150.0 0.8 pad_maximum_fusion.12
  150.9 2.1 %add_bitcast_fusion = f32[1,4096,128]{2,1,0:T(8,128)} fusion(f32[4096,128]{1,0:T(8,128)S(1)} %copy-done.5, f32[1,4096,128]{2,1,0:T(8,128)S(1)} %copy-done.2, f32[128]{0:T(128)S(1)} %get-tuple-element.40, f32[128]{0:T(128)S(1)} %get-tuple-element.41, f32[128]{0:T(128)S(1)} %get-tuple-element.42, f32[128]{0:T(128)S(1)} %get-tuple-element.39, ...), kind=kLoop, calls=%fused_computation.56 | loop fusion | flops 5767168 | bytes 6294528 | tf_op jit(solution)/shard_map/broadcast_in_dim | solution.py:484
  (57 shorter events, 0.5 us)
Async XLA Ops:
  0.6 42.2 %copy-start = (bf16[256,128]{1,0:T(8,128)(2,1)S(1)}, bf16[256,128]{1,0:T(8,128)(2,1)}, u32[]{:S(2)}) copy-start(bf16[256,128]{1,0:T(8,128)(2,1)} %param.17) | copy-start | bytes 196612
  0.7 2.3 %copy-start.2 = (f32[1,4096,128]{2,1,0:T(8,128)S(1)}, f32[1,4096,128]{2,1,0:T(8,128)}, u32[]{:S(2)}) copy-start(f32[1,4096,128]{2,1,0:T(8,128)} %param.10) | copy-start | bytes 6291460
  0.7 21.7 %copy-start.12 = (f32[128]{0:T(128)S(1)}, f32[128]{0:T(128)}, u32[]{:S(2)}) copy-start(f32[128]{0:T(128)} %param.18) | copy-start | bytes 1540
  0.7 21.7 %copy-start.14 = (f32[128]{0:T(128)S(1)}, f32[128]{0:T(128)}, u32[]{:S(2)}) copy-start(f32[128]{0:T(128)} %param.19) | copy-start | bytes 1540
  0.7 21.7 %copy-start.10 = (bf16[128,128]{1,0:T(8,128)(2,1)S(1)}, bf16[128,128]{1,0:T(8,128)(2,1)}, u32[]{:S(2)}) copy-start(bf16[128,128]{1,0:T(8,128)(2,1)} %param.12) | copy-start | bytes 98308
  3.6 23.1 %copy-start.8 = (bf16[2,2,128,256]{3,2,1,0:T(8,128)(2,1)S(1)}, bf16[2,2,128,256]{3,2,1,0:T(8,128)(2,1)}, u32[]{:S(2)}) copy-start(bf16[2,2,128,256]{3,2,1,0:T(8,128)(2,1)} %param.13) | copy-start | bytes 786436
  22.9 12.5 %copy-start.3 = (bf16[4096,128]{1,0:T(8,128)(2,1)}, bf16[4096,128]{1,0:T(8,128)(2,1)S(1)}, u32[]{:S(2)}) copy-start(bf16[4096,128]{1,0:T(8,128)(2,1)S(1)} %convolution_convert_fusion) | copy-start | bytes 3145732
  23.6 5.7 %copy-start.13 = (f32[2,256]{1,0:T(2,128)S(1)}, f32[2,256]{1,0:T(2,128)}, u32[]{:S(2)}) copy-start(f32[2,256]{1,0:T(2,128)} %param.14) | copy-start | bytes 6148
  23.6 8.0 %collective-permute-start = (bf16[256,128]{1,0:T(8,128)(2,1)}, bf16[256,128]{1,0:T(8,128)(2,1)}, u32[]{:S(2)}, u32[]{:S(2)}) collective-permute-start(bf16[256,128]{1,0:T(8,128)(2,1)} %slice.215), channel_id=1, source_target_pairs={{0,1},{1,2},{2,3},{3,4},{4,5},{5,6},{6,7},{7,8},{8,9},{9,10},{10,1... | collective-permute-start | bytes 196616 | tf_op jit(solution)/shard_map/ppermute | solution.py:20
  34.5 0.9 copy-start.11
  35.9 2.8 %copy-start.9 = (bf16[2,128,256]{2,1,0:T(8,128)(2,1)S(1)}, bf16[2,128,256]{2,1,0:T(8,128)(2,1)}, u32[]{:S(2)}) copy-start(bf16[2,128,256]{2,1,0:T(8,128)(2,1)} %param.16) | copy-start | bytes 393220
  36.6 3.8 %collective-permute-start.1 = (bf16[512,128]{1,0:T(8,128)(2,1)S(1)}, bf16[512,128]{1,0:T(8,128)(2,1)S(1)}, u32[]{:S(2)}, u32[]{:S(2)}) collective-permute-start(bf16[512,128]{1,0:T(8,128)(2,1)S(1)} %slice.218), channel_id=1, source_target_pairs={{0,1},{1,2},{2,3},{3,4},{4,5},{5,6},{6,7},{7,8},{8,9},{9,10},{10,1... | collective-permute-start | bytes 393224 | tf_op jit(solution)/shard_map/ppermute | solution.py:20
  42.0 1.6 %copy-start.7 = (f32[1,4096,128]{2,1,0:T(8,128)S(1)}, f32[1,4096,128]{2,1,0:T(8,128)}, u32[]{:S(2)}) copy-start(f32[1,4096,128]{2,1,0:T(8,128)} %param.11) | copy-start | bytes 6291460
  54.3 7.5 %collective-permute-start.2 = (bf16[512,256]{0,1:T(8,128)(2,1)S(1)}, bf16[512,256]{0,1:T(8,128)(2,1)S(1)}, u32[]{:S(2)}, u32[]{:S(2)}) collective-permute-start(bf16[512,256]{0,1:T(8,128)(2,1)S(1)} %slice.221), channel_id=1, source_target_pairs={{1,0},{2,1},{3,2},{4,3},{5,4},{6,5},{7,6},{8,7},{9,8},{10,9},{11,1... | collective-permute-start | bytes 786440 | tf_op jit(solution)/shard_map/ppermute | solution.py:20
  64.0 1.2 copy-start.4
  70.4 6.2 %collective-permute-start.3 = (bf16[256,256]{0,1:T(8,128)(2,1)S(1)}, bf16[256,256]{0,1:T(8,128)(2,1)S(1)}, u32[]{:S(2)}, u32[]{:S(2)}) collective-permute-start(bf16[256,256]{0,1:T(8,128)(2,1)S(1)} %slice.222), channel_id=1, source_target_pairs={{1,0},{2,1},{3,2},{4,3},{5,4},{6,5},{7,6},{8,7},{9,8},{10,9},{11,1... | collective-permute-start | bytes 393224 | tf_op jit(solution)/shard_map/ppermute | solution.py:20
  77.4 2.0 %copy-start.6 = (bf16[4096,128]{1,0:T(8,128)(2,1)}, bf16[4096,128]{1,0:T(8,128)(2,1)S(1)}, u32[]{:S(2)}) copy-start(bf16[4096,128]{1,0:T(8,128)(2,1)S(1)} %fusion.6) | copy-start | bytes 3145732
  149.2 1.7 %copy-start.5 = (f32[4096,128]{1,0:T(8,128)S(1)}, f32[4096,128]{1,0:T(8,128)}, u32[]{:S(2)}) copy-start(f32[4096,128]{1,0:T(8,128)} %get-tuple-element.45) | copy-start | bytes 6291460
  150.9 2.1 %copy-start.1 = (bf16[256,128]{1,0:T(8,128)(2,1)S(1)}, bf16[256,128]{1,0:T(8,128)(2,1)}, u32[]{:S(2)}) copy-start(bf16[256,128]{1,0:T(8,128)(2,1)} %param.17) | copy-start | bytes 196612

commit v2 on v0

v2 whole, which is shorter than its diff:
```python
import jax
import jax.numpy as jnp
from jax import lax
from jax.experimental import pallas as pl
from jax.experimental.pallas import tpu as pltpu
from jax.sharding import PartitionSpec as P

FIRST = 256
SECOND = 512
TM = 32
SER = 8
X = 4
Z = 8
GROUP = X * SER
ROWS = 512
MESH = pl.DeviceIdType.MESH
EARLY, LATE, LAST = 40, 24, 8

epsilon = 1e-05
gelu_coeff = 0.7978845608
cubic_coeff = 0.044715


def nn(left, right):
    return jnp.dot(left, right, preferred_element_type=jnp.float32)


def nt(left, right):
    return lax.dot_general(
        left, right, (((1,), (1,)), ((), ())), preferred_element_type=jnp.float32
    )


def tn(left, right):
    return lax.dot_general(
        left, right, (((0,), (0,)), ((), ())), preferred_element_type=jnp.float32
    )


def fold(values):
    return jnp.sum(values.reshape(-1, 8, values.shape[-1]), axis=0)


def each(lo, hi, body):
    def run(k, carry):
        body(k)
        return carry

    lax.fori_loop(lo, hi, run, 0)


def at(start, size):
    return pl.ds(pl.multiple_of(start, 8), size)


def remote(src, dst, s_sem, r_sem, device):
    return pltpu.make_async_remote_copy(
        src_ref=src,
        dst_ref=dst,
        send_sem=s_sem,
        recv_sem=r_sem,
        device_id=device,
        device_id_type=MESH,
    )


def block_kernel(
    x_hbm,
    cot_hbm,
    w_in,
    w_conv,
    bias,
    w_res,
    w_skip,
    w_out,
    gain_ref,
    offset_ref,
    grad_hbm,
    early_out,
    late_out,
    last_out,
    x,
    cot,
    level_zero,
    level_one,
    gated_one,
    tanh_one,
    sigm_one,
    incoming_one,
    near_one,
    far_one,
    near_zero,
    far_zero,
    hat,
    early,
    late,
    last,
    in_grad,
    acc,
    stats,
    stats_all,
    ends,
    ends_all,
    early_one,
    late_one,
    last_one,
    early_two,
    late_two,
    last_two,
    early_block,
    late_block,
    last_block,
    load_sem,
    store_sem,
    halo_s,
    halo_r,
    stats_s,
    stats_r,
    ends_s,
    ends_r,
    one_s,
    one_r,
    two_s,
    two_r,
    three_s,
    three_r,
):
    steps = x.shape[0]
    chunks = steps // ROWS
    total_steps = float(steps * TM)
    ser = lax.axis_index("series")
    tm = lax.axis_index("tm")
    place, depth = tm // Z, lax.rem(tm, Z)
    mine = place * SER + ser

    def member(p):
        return {"series": lax.rem(p, SER), "tm": (p // SER) * Z + depth}

    def load_x(c):
        return pltpu.make_async_copy(
            x_hbm.at[at(c * ROWS, ROWS)], x.at[at(c * ROWS, ROWS)], load_sem.at[c]
        )

    load_cot = pltpu.make_async_copy(cot_hbm, cot, load_sem.at[chunks])
    each(0, chunks, lambda c: load_x(c).start())
    load_cot.start()

    barrier = pltpu.get_barrier_semaphore()

    def hello(device):
        pl.semaphore_signal(barrier, inc=1, device_id=device, device_id_type=MESH)

    each(1, TM, lambda k: hello({"tm": lax.rem(tm + k, TM)}))
    each(1, GROUP, lambda k: hello(member(lax.rem(mine + k, GROUP))))

    acc[...] = jnp.zeros_like(acc)
    early[...] = jnp.zeros_like(early)
    late[...] = jnp.zeros_like(late)
    last[...] = jnp.zeros_like(last)
    in_grad[...] = jnp.zeros_like(in_grad)

    @pl.when(tm == 0)
    def _():
        level_zero[pl.ds(0, FIRST)] = jnp.zeros((FIRST, 128), jnp.bfloat16)
        level_one[pl.ds(0, SECOND)] = jnp.zeros((SECOND, 128), jnp.bfloat16)

    @pl.when(tm == TM - 1)
    def _():
        far_one[pl.ds(steps, SECOND)] = jnp.zeros((SECOND, 128), jnp.float32)
        far_zero[pl.ds(steps, FIRST)] = jnp.zeros((FIRST, 128), jnp.float32)

    def sum_x(c):
        load_x(c).wait()
        acc[0] += fold(x[at(c * ROWS, ROWS)])

    each(0, chunks, sum_x)
    local_sum = jnp.sum(acc[0], axis=0, keepdims=True)
    local_mean = local_sum / steps

    def sum_squares(c):
        centred = x[at(c * ROWS, ROWS)] - local_mean
        acc[1] += fold(centred * centred)

    each(0, chunks, sum_squares)
    stats[0:1] = local_sum
    stats[1:2] = jnp.sum(acc[1], axis=0, keepdims=True)
    stats_all[pl.ds(tm, 1)] = stats[...][None]

    pl.semaphore_wait(barrier, TM + GROUP - 2)

    def spread_copy(src, dst, s_sem, r_sem, peer, slot):
        return remote(src, dst.at[slot], s_sem.at[peer], r_sem.at[slot], {"tm": peer})

    def stats_copy(peer, slot):
        return spread_copy(stats, stats_all, stats_s, stats_r, peer, slot)

    def ends_copy(peer, slot):
        return spread_copy(ends, ends_all, ends_s, ends_r, peer, slot)

    each(1, TM, lambda k: stats_copy(lax.rem(tm + k, TM), tm).start())

    def take_stats(k):
        peer = lax.rem(tm + k, TM)
        stats_copy(peer, peer).wait()

    each(1, TM, take_stats)

    sums, squares = stats_all[:, 0], stats_all[:, 1]
    mean = jnp.sum(sums, axis=0, keepdims=True) / total_steps
    shift = sums / steps - mean
    variance = (
        jnp.sum(squares, axis=0, keepdims=True)
        + steps * jnp.sum(shift * shift, axis=0, keepdims=True)
    ) / total_steps
    inverse = lax.rsqrt(variance + epsilon)
    spread = jnp.sqrt(variance + epsilon)
    gain, offset = gain_ref[...], offset_ref[...]
    scale = spread / gain

    later, earlier = {"tm": lax.rem(tm + 1, TM)}, {"tm": lax.rem(tm + TM - 1, TM)}
    halo = (
        remote(
            level_zero.at[pl.ds(steps, FIRST)],
            level_zero.at[pl.ds(0, FIRST)],
            halo_s.at[0],
            halo_r.at[0],
            later,
        ),
        remote(
            level_one.at[pl.ds(steps, SECOND)],
            level_one.at[pl.ds(0, SECOND)],
            halo_s.at[1],
            halo_r.at[1],
            later,
        ),
        remote(
            far_one.at[pl.ds(0, SECOND)],
            far_one.at[pl.ds(steps, SECOND)],
            halo_s.at[2],
            halo_r.at[2],
            earlier,
        ),
        remote(
            far_zero.at[pl.ds(0, FIRST)],
            far_zero.at[pl.ds(steps, FIRST)],
            halo_s.at[3],
            halo_r.at[3],
            earlier,
        ),
    )

    def normalize(c):
        hat_x = (x[at(c * ROWS, ROWS)] - mean) * inverse
        return hat_x, (hat_x * gain + offset).astype(jnp.bfloat16)

    def project(i):
        c = chunks - 1 - i
        _, normed = normalize(c)
        level_zero[at(FIRST + c * ROWS, ROWS)] = nn(normed, w_in[...]).astype(jnp.bfloat16)

        @pl.when(jnp.logical_and(i == 0, tm < TM - 1))
        def _():
            halo[0].start()

    each(0, chunks, project)

    def gates(act):
        return jnp.tanh(act[:, :128]), 0.5 * jnp.tanh(0.5 * act[:, 128:]) + 0.5

    def window_zero(c):
        return jnp.concatenate(
            [level_zero[at(c * ROWS, ROWS)], level_zero[at(c * ROWS + FIRST, ROWS)]], axis=1
        )

    def window_one(c):
        return jnp.concatenate(
            [level_one[at(c * ROWS, ROWS)], level_one[at(c * ROWS + SECOND, ROWS)]], axis=1
        )

    def layer_one(i):
        c = chunks - 1 - i

        @pl.when(jnp.logical_and(c == 0, tm > 0))
        def _():
            halo[0].wait_recv()

        now = at(c * ROWS, ROWS)
        tanh, sigm = gates(nn(window_zero(c), w_conv[0]) + bias[0:1])
        gated = (tanh * sigm).astype(jnp.bfloat16)
        tanh_one[now] = tanh
        sigm_one[now] = sigm
        gated_one[now] = gated
        level = level_zero[at(c * ROWS + FIRST, ROWS)].astype(jnp.float32)
        level_one[at(c * ROWS + SECOND, ROWS)] = (level + nn(gated, w_res[...])).astype(
            jnp.bfloat16
        )

        @pl.when(jnp.logical_and(i == 0, tm < TM - 1))
        def _():
            halo[1].start()

    each(0, chunks, layer_one)

    def gate_back(incoming, tanh, sigm):
        part = incoming * sigm
        return part * (1.0 - tanh * tanh), part * tanh * (1.0 - sigm)

    load_cot.wait()

    @pl.when(tm > 0)
    def _():
        halo[1].wait_recv()

    def layer_two(c):
        now = at(c * ROWS, ROWS)
        window = window_one(c)
        tanh, sigm = gates(nn(window, w_conv[1]) + bias[1:2])
        gated = (tanh * sigm).astype(jnp.bfloat16)
        both = jnp.concatenate([gated_one[now], gated], axis=1)
        skip = nn(both, w_skip[...])
        square = skip * skip
        half = 0.5 * jnp.tanh(
            skip * (gelu_coeff + (gelu_coeff * cubic_coeff) * square)
        ) + 0.5
        value = skip * half
        slope = half + value * (1.0 - half) * (
            2.0 * gelu_coeff + (6.0 * gelu_coeff * cubic_coeff) * square
        )
        rectified = value.astype(jnp.bfloat16)
        forecast = nn(rectified, w_out[...])
        gradient = cot[now]
        acc[2] += fold(gradient)
        acc[3] += fold(gradient * (forecast - offset))
        scaled = (gradient * scale).astype(jnp.bfloat16)
        out_part = tn(rectified, scaled)
        early[1024:1152] += out_part[:128]
        late[640:768] += out_part[128:]
        back_skip = (nt(scaled, w_out[...]) * slope).astype(jnp.bfloat16)
        skip_part = tn(both, back_skip)
        early[512:768] += skip_part[:, :128]
        early[768:1024] += skip_part[:, 128:]
        incoming = nt(back_skip, w_skip[...])
        incoming_one[now] = incoming[:, :128]
        first, second = gate_back(incoming[:, 128:], tanh, sigm)
        acc[4] += fold(first)
        acc[5] += fold(second)
        pre = jnp.concatenate([first, second], axis=1).astype(jnp.bfloat16)
        conv_part = tn(window, pre)
        early[0:256] += conv_part[:, :128]
        early[256:512] += conv_part[:, 128:]
        carried = nt(pre, w_conv[1])
        far_one[now] = carried[:, :128]
        near_one[now] = carried[:, 128:]

        @pl.when(jnp.logical_and(c == 0, tm > 0))
        def _():
            halo[2].start()

    each(0, chunks, layer_two)

    def one(g, src, dst, size, peer, slot):
        return remote(
            src.at[at(peer * size, size)],
            dst.at[slot],
            one_s.at[g, peer],
            one_r.at[g, slot],
            member(peer),
        )

    def two(g, src, dst, peer, slot):
        return remote(
            src, dst.at[slot], two_s.at[g, peer], two_r.at[g, slot], {"tm": place * Z + peer}
        )

    def three(g, out, size, peer, slot):
        where = out.at[at(slot * size, size)]
        return remote(where, where, three_s.at[g, peer], three_r.at[g, slot], member(peer))

    groups = (
        (early, early_one, early_block, early_two, early_out, EARLY),
        (late, late_one, late_block, late_two, late_out, LATE),
        (last, last_one, last_block, last_two, last_out, LAST),
    )

    def scatter(g):
        src, dst, block, _, _, size = groups[g]
        each(1, GROUP, lambda k: one(g, src, dst, size, lax.rem(mine + k, GROUP), mine).start())
        dst[pl.ds(mine, 1)] = src[at(mine * size, size)][None]

    def middle(g):
        src, dst, block, far, _, size = groups[g]

        def take(k):
            peer = lax.rem(mine + k, GROUP)
            one(g, src, dst, size, peer, peer).wait()

        each(1, GROUP, take)
        total = dst[0]
        for p in range(1, GROUP):
            total = total + dst[p]
        block[...] = total
        each(1, Z, lambda k: two(g, block, far, lax.rem(depth + k, Z), depth).start())
        far[pl.ds(depth, 1)] = total[None]

    def gather(g):
        _, _, block, far, out, size = groups[g]

        def take(k):
            peer = lax.rem(depth + k, Z)
            two(g, block, far, peer, peer).wait()

        each(1, Z, take)
        total = far[0]
        for z in range(1, Z):
            total = total + far[z]
        out[at(mine * size, size)] = total
        each(1, GROUP, lambda k: three(g, out, size, lax.rem(mine + k, GROUP), mine).start())

    def finish(g):
        _, _, _, _, out, size = groups[g]

        def take(k):
            peer = lax.rem(mine + k, GROUP)
            three(g, out, size, peer, mine).wait_send()
            three(g, out, size, peer, peer).wait_recv()

        each(1, GROUP, take)

    scatter(0)

    def back_one(c):
        @pl.when(jnp.logical_and(c == chunks - 1, tm < TM - 1))
        def _():
            halo[2].wait_recv()

        now = at(c * ROWS, ROWS)
        arrived = near_one[now] + far_one[at(c * ROWS + SECOND, ROWS)]
        grad_one = arrived.astype(jnp.bfloat16)
        late[512:640] += tn(gated_one[now], grad_one)
        incoming = incoming_one[now] + nt(grad_one, w_res[...])
        first, second = gate_back(incoming, tanh_one[now], sigm_one[now])
        acc[6] += fold(first)
        acc[7] += fold(second)
        pre = jnp.concatenate([first, second], axis=1).astype(jnp.bfloat16)
        conv_part = tn(window_zero(c), pre)
        late[0:256] += conv_part[:, :128]
        late[256:512] += conv_part[:, 128:]
        carried = nt(pre, w_conv[0])
        far_zero[now] = carried[:, :128]
        near_zero[now] = grad_one.astype(jnp.float32) + carried[:, 128:]

        @pl.when(jnp.logical_and(c == 0, tm > 0))
        def _():
            halo[3].start()

    each(0, chunks, back_one)
    scatter(1)
    middle(0)

    def back_zero(c):
        @pl.when(jnp.logical_and(c == chunks - 1, tm < TM - 1))
        def _():
            halo[3].wait_recv()

        now = at(c * ROWS, ROWS)
        grad_zero = (near_zero[now] + far_zero[at(c * ROWS + FIRST, ROWS)]).astype(jnp.bfloat16)
        hat_x, normed = normalize(c)
        in_grad[...] += tn(normed, grad_zero)
        grad_hat = nt(grad_zero, w_in[...]) * gain
        hat[now] = grad_hat
        acc[8] += fold(grad_hat)
        acc[9] += fold(grad_hat * hat_x)

    each(0, chunks, back_zero)

    def column(k):
        return jnp.sum(acc[k], axis=0, keepdims=True)

    sum_a, sum_b, out_a, out_b = column(8), column(9), column(2), column(3) / gain
    ends[0:1] = sum_a
    ends[1:2] = sum_b
    ends[2:3] = out_a
    ends[3:4] = out_b
    each(1, TM, lambda k: ends_copy(lax.rem(tm + k, TM), tm).start())
    ends_all[pl.ds(tm, 1)] = ends[...][None]
    for p in range(GROUP):
        last[8 * p : 8 * p + 4] = in_grad[4 * p : 4 * p + 4]
    last[4:5] = (sum_b - out_b * spread) / gain
    last[12:13] = (sum_a - out_a * spread) / gain
    last[20:21] = column(6)
    last[28:29] = column(7)
    last[36:37] = column(4)
    last[44:45] = column(5)
    scatter(2)
    gather(0)
    middle(1)

    def take_ends(k):
        peer = lax.rem(tm + k, TM)
        ends_copy(peer, peer).wait()

    each(1, TM, take_ends)
    totals = jnp.sum(ends_all[...], axis=0) / total_steps
    slant = inverse * (totals[3:4] - inverse * totals[1:2])
    level = totals[2:3] - inverse * totals[0:1]
    middle(2)

    def store(c):
        return pltpu.make_async_copy(
            hat.at[at(c * ROWS, ROWS)], grad_hbm.at[at(c * ROWS, ROWS)], store_sem.at[c]
        )

    def resolve(c):
        now = at(c * ROWS, ROWS)
        hat[now] = hat[now] * inverse + ((x[now] - mean) * slant + level)
        store(c).start()

    each(0, chunks, resolve)
    gather(1)
    gather(2)

    @pl.when(tm < TM - 1)
    def _():
        halo[0].wait_send()
        halo[1].wait_send()

    @pl.when(tm > 0)
    def _():
        halo[2].wait_send()
        halo[3].wait_send()

    each(0, chunks, lambda c: store(c).wait())
    finish(0)
    finish(1)
    finish(2)


def unpack_kernel(early, late, last, conv, bias, res, skip, out, into, gain, shift):
    for layer, src in ((0, late), (1, early)):
        for tap in range(2):
            for half in range(2):
                conv[layer, tap, :, half * 128 : half * 128 + 128] = src[
                    pl.ds(half * 256 + tap * 128, 128)
                ]
    for layer in range(2):
        for half in range(2):
            skip[layer, :, half * 128 : half * 128 + 128] = early[
                pl.ds(512 + half * 256 + layer * 128, 128)
            ]
            bias[layer : layer + 1, half * 128 : half * 128 + 128] = last[
                pl.ds(20 + layer * 16 + half * 8, 1)
            ]
    out[0:128] = early[1024:1152]
    out[128:256] = late[640:768]
    res[...] = late[512:640]
    for p in range(GROUP):
        into[4 * p : 4 * p + 4] = last[8 * p : 8 * p + 4]
    gain[...] = last[4:5]
    shift[...] = last[12:13]


def on_device(
    series_data,
    cotangent,
    in_weight,
    convolution_weight,
    convolution_bias,
    res_weight,
    skip_weight,
    output_weight,
    norm_gain_vector,
    norm_offset_vector,
):
    steps = series_data.shape[1]
    f32, bf16 = jnp.float32, jnp.bfloat16
    vmem = pl.BlockSpec(memory_space=pltpu.VMEM)
    hbm = pl.BlockSpec(memory_space=pl.ANY)
    sem = pltpu.SemaphoreType.DMA
    shape = jax.ShapeDtypeStruct
    field = pltpu.VMEM((steps, 128), f32)

    def sizes(lead):
        return [pltpu.VMEM((lead, size, 128), f32) for size in (EARLY, LATE, LAST)]

    grad, early, late, last = pl.pallas_call(
        block_kernel,
        name="block",
        out_shape=(
            shape((steps, 128), f32),
            shape((GROUP * EARLY, 128), f32),
            shape((GROUP * LATE, 128), f32),
            shape((GROUP * LAST, 128), f32),
        ),
        in_specs=[hbm, hbm] + [vmem] * 8,
        out_specs=(hbm, vmem, vmem, vmem),
        scratch_shapes=[
            field,
            field,
            pltpu.VMEM((steps + FIRST, 128), bf16),
            pltpu.VMEM((steps + SECOND, 128), bf16),
            pltpu.VMEM((steps, 128), bf16),
            field,
            field,
            field,
            field,
            pltpu.VMEM((steps + SECOND, 128), f32),
            field,
            pltpu.VMEM((steps + FIRST, 128), f32),
            field,
            pltpu.VMEM((GROUP * EARLY, 128), f32),
            pltpu.VMEM((GROUP * LATE, 128), f32),
            pltpu.VMEM((GROUP * LAST, 128), f32),
            pltpu.VMEM((128, 128), f32),
            pltpu.VMEM((10, 8, 128), f32),
            pltpu.VMEM((2, 128), f32),
            pltpu.VMEM((TM, 2, 128), f32),
            pltpu.VMEM((4, 128), f32),
            pltpu.VMEM((TM, 4, 128), f32),
            *sizes(GROUP),
            *sizes(Z),
            pltpu.VMEM((EARLY, 128), f32),
            pltpu.VMEM((LATE, 128), f32),
            pltpu.VMEM((LAST, 128), f32),
            sem((steps // ROWS + 1,)),
            sem((steps // ROWS,)),
            sem((4,)),
            sem((4,)),
            sem((TM,)),
            sem((TM,)),
            sem((TM,)),
            sem((TM,)),
            sem((3, GROUP)),
            sem((3, GROUP)),
            sem((3, Z)),
            sem((3, Z)),
            sem((3, GROUP)),
            sem((3, GROUP)),
        ],
        compiler_params=pltpu.CompilerParams(
            collective_id=0, has_side_effects=True, vmem_limit_bytes=60 * 1024 * 1024
        ),
    )(
        series_data[0],
        cotangent[0],
        in_weight,
        convolution_weight.reshape(2, 256, 256),
        convolution_bias,
        res_weight,
        skip_weight.reshape(256, 256),
        output_weight,
        norm_gain_vector.reshape(1, 128),
        norm_offset_vector.reshape(1, 128),
    )
    conv, bias, res, skip, out, into, gain, shift = pl.pallas_call(
        unpack_kernel,
        name="unpack",
        out_shape=(
            shape((2, 2, 128, 256), f32),
            shape((2, 256), f32),
            shape((128, 128), f32),
            shape((2, 128, 256), f32),
            shape((256, 128), f32),
            shape((128, 128), f32),
            shape((1, 128), f32),
            shape((1, 128), f32),
        ),
        in_specs=[vmem] * 3,
        out_specs=(vmem,) * 8,
    )(early, late, last)
    return grad[None], conv, bias, res, skip, out, into, gain.reshape(128), shift.reshape(128)


def solution(mesh):
    split = P("series", "tm", None)
    return jax.shard_map(
        on_device,
        mesh=mesh,
        in_specs=(split, split) + (P(),) * 8,
        out_specs=(split,) + (P(),) * 8,
        check_vma=False,
    )
```

time: 556 us -> 81.3 us (0.15)
  blocking collectives: 298 us -> 0 us
  waiting for transfers between devices: 179 us -> 0 us
  Pallas kernels: 0 us -> 77.5 us
  matrix products: 32.3 us -> 0 us
  other arithmetic: 16.1 us -> 0 us
  between operations: 14.4 us -> 0.65 us
  starting transfers between devices: 8.1 us -> 0 us
    psum x4 -> x0, blocking collectives: 298 us -> none  [the longest x1 120 us: on_device(): lax.psum((first_convolved, second_convolved, bias_one, bias_two, res_grad...]
    psum x1 -> x0, waiting for transfers between devices: 173 us -> none  [on_device(): lax.psum((first_convolved, second_convolved, bias_one, bias_two, res_grad...]
    pallas_call x0 -> x2, Pallas kernels: none -> 77.5 us  [the longest x1 75.2 us: on_device(): pl.pallas_call(block_kernel, name='block', out_shape=(shape((steps, 128),...]
    dot_general x27 -> x0, matrix products: 32.3 us -> none  [the longest x9 12 us: transposed_product(): lax.dot_general(left, right, (((1,), (1,)), ((), ())), preferred_element_...]
    ppermute x4 -> x0, starting transfers between devices: 8.06 us -> none  [shifted(): return lax.ppermute(block, axis, route)]
    ppermute x4 -> x0, waiting for transfers between devices: 5.7 us -> none  [shifted(): return lax.ppermute(block, axis, route)]
  transfers between devices with their start and end apart: 5 -> 0, of which waited for: 4 -> 0; matrix products, arithmetic and copies ran while one was open for 3% -> 0% of each run, Pallas kernels for 0% -> 0%
where the time goes in v2:
time: 81.3 us; the launch traced here: 81.2 us
  Pallas kernels  77.5 us (95%)
  local copies, waits for them, and re-layouts  3.05 us (4%)
    pallas_call x1, Pallas kernels, on_device(): pl.pallas_call(block_kernel, name='block', out_shape=(shape((steps, 128),...  75.2 us
    unnamed x1, local copies, waits for them, and re-layouts  3.05 us
    pallas_call x1, Pallas kernels, on_device(): pl.pallas_call(unpack_kernel, name='unpack', out_shape=(shape((2, 2, 128,...  2.21 us

profile of v2, /device:TPU:1, one launch (start us, length us, event | category | flops | bytes accessed | tf_op | source)
XLA Modules:
  0.0 81.2 jit_solution(3207239442613322949)
XLA Ops:
  0.6 75.2 %block.1 = (f32[4096,128]{1,0:T(8,128)}, f32[1280,128]{1,0:T(8,128)}, f32[768,128]{1,0:T(8,128)}, f32[256,128]{1,0:T(8,128)}) custom-call(f32[4096,128]{1,0:T(8,128)} %bitcast.9, f32[4096,128]{1,0:T(8,128)} %bitcast.10, bf16[128,128]{1,0:T(8,128)(2,1)} %w_in.1, bf16[2,256,256]{2,1,0:T(8,128)(2,1)} %bitcast.12, f32[2,256]{1,0:T(2,128)} %bias.1, ...), custom_call_target="tpu_custom_call" | custom-call | tf_op jit(solution)/shard_map/block/pallas_call | solution.py:585
  75.9 2.2 %unpack.1 = (f32[2,2,128,256]{3,2,1,0:T(8,128)}, f32[2,256]{1,0:T(2,128)}, f32[128,128]{1,0:T(8,128)}, f32[2,128,256]{2,1,0:T(8,128)}, f32[256,128]{1,0:T(8,128)...) custom-call(f32[1280,128]{1,0:T(8,128)} %get-tuple-element.22.early, ...), custom_call_target="tpu_custom_call" | custom-call | tf_op jit(solution)/shard_map/unpack/pallas_call | solution.py:654
  78.1 3.0 %copy.20 = f32[1,4096,128]{2,1,0:T(8,128)} copy(f32[1,4096,128]{2,1,0:T(8,128)} %bitcast.11) | data formatting | bytes 4194304

commit v3 on v2

--- a/solution.py
+++ b/solution.py
@@ -11,7 +11,9 @@
 SER = 8
 X = 4
 Z = 8
-GROUP = X * SER
+Y = 4
+PLANE = X * Y
+PARTS = 2 * PLANE
 ROWS = 512
 MESH = pl.DeviceIdType.MESH
 EARLY, LATE, LAST = 40, 24, 8
@@ -67,6 +69,18 @@
 def block_kernel(
     x_hbm,
     cot_hbm,
+    w_in_hbm,
+    w_conv_hbm,
+    bias_hbm,
+    w_res_hbm,
+    w_skip_hbm,
+    w_out_hbm,
+    gain_hbm,
+    offset_hbm,
+    hat,
+    early_out,
+    late_out,
+    last_out,
     w_in,
     w_conv,
     bias,
@@ -75,10 +89,6 @@
     w_out,
     gain_ref,
     offset_ref,
-    grad_hbm,
-    early_out,
-    late_out,
-    last_out,
     x,
     cot,
     level_zero,
@@ -91,16 +101,23 @@
     far_one,
     near_zero,
     far_zero,
-    hat,
     early,
     late,
     last,
     in_grad,
     acc,
     stats,
-    stats_all,
+    stats_z,
+    stats_x,
     ends,
-    ends_all,
+    ends_z,
+    ends_x,
+    early_pair,
+    late_pair,
+    last_pair,
+    early_half,
+    late_half,
+    last_half,
     early_one,
     late_one,
     last_one,
@@ -111,30 +128,39 @@
     late_block,
     last_block,
     load_sem,
-    store_sem,
     halo_s,
     halo_r,
-    stats_s,
-    stats_r,
-    ends_s,
-    ends_r,
+    line_s,
+    line_r,
+    pair_s,
+    pair_r,
     one_s,
     one_r,
     two_s,
     two_r,
     three_s,
     three_r,
+    back_s,
+    back_r,
 ):
     steps = x.shape[0]
     chunks = steps // ROWS
     total_steps = float(steps * TM)
     ser = lax.axis_index("series")
     tm = lax.axis_index("tm")
-    place, depth = tm // Z, lax.rem(tm, Z)
-    mine = place * SER + ser
-
-    def member(p):
-        return {"series": lax.rem(p, SER), "tm": (p // SER) * Z + depth}
+    across, depth = tm // Z, lax.rem(tm, Z)
+    up, core = ser // 2, lax.rem(ser, 2)
+    mine = across * Y + up
+    mate = {"series": ser + 1 - 2 * core}
+
+    def on_z(peer):
+        return {"tm": across * Z + peer}
+
+    def on_x(peer):
+        return {"tm": peer * Z + depth}
+
+    def on_plane(peer):
+        return {"series": lax.rem(peer, Y) * 2 + core, "tm": (peer // Y) * Z + depth}
 
     def load_x(c):
         return pltpu.make_async_copy(
@@ -144,14 +170,36 @@
     load_cot = pltpu.make_async_copy(cot_hbm, cot, load_sem.at[chunks])
     each(0, chunks, lambda c: load_x(c).start())
     load_cot.start()
+    params = [
+        pltpu.make_async_copy(src, dst, load_sem.at[chunks + 1 + k])
+        for k, (src, dst) in enumerate(
+            (
+                (w_in_hbm, w_in),
+                (w_conv_hbm, w_conv),
+                (bias_hbm, bias),
+                (w_res_hbm, w_res),
+                (w_skip_hbm, w_skip),
+                (w_out_hbm, w_out),
+                (gain_hbm, gain_ref),
+                (offset_hbm, offset_ref),
+            )
+        )
+    ]
+    for copy in params:
+        copy.start()
 
     barrier = pltpu.get_barrier_semaphore()
 
     def hello(device):
         pl.semaphore_signal(barrier, inc=1, device_id=device, device_id_type=MESH)
 
-    each(1, TM, lambda k: hello({"tm": lax.rem(tm + k, TM)}))
-    each(1, GROUP, lambda k: hello(member(lax.rem(mine + k, GROUP))))
+    for k in range(1, Z):
+        hello(on_z(lax.rem(depth + k, Z)))
+    for k in range(1, X):
+        hello(on_x(lax.rem(across + k, X)))
+    for k in range(1, Y):
+        hello({"series": lax.rem(up + k, Y) * 2 + core})
+    hello(mate)
 
     acc[...] = jnp.zeros_like(acc)
     early[...] = jnp.zeros_like(early)
@@ -184,36 +232,38 @@
     each(0, chunks, sum_squares)
     stats[0:1] = local_sum
     stats[1:2] = jnp.sum(acc[1], axis=0, keepdims=True)
-    stats_all[pl.ds(tm, 1)] = stats[...][None]
-
-    pl.semaphore_wait(barrier, TM + GROUP - 2)
-
-    def spread_copy(src, dst, s_sem, r_sem, peer, slot):
-        return remote(src, dst.at[slot], s_sem.at[peer], r_sem.at[slot], {"tm": peer})
-
-    def stats_copy(peer, slot):
-        return spread_copy(stats, stats_all, stats_s, stats_r, peer, slot)
-
-    def ends_copy(peer, slot):
-        return spread_copy(ends, ends_all, ends_s, ends_r, peer, slot)
-
-    each(1, TM, lambda k: stats_copy(lax.rem(tm + k, TM), tm).start())
-
-    def take_stats(k):
-        peer = lax.rem(tm + k, TM)
-        stats_copy(peer, peer).wait()
-
-    each(1, TM, take_stats)
-
-    sums, squares = stats_all[:, 0], stats_all[:, 1]
-    mean = jnp.sum(sums, axis=0, keepdims=True) / total_steps
-    shift = sums / steps - mean
-    variance = (
-        jnp.sum(squares, axis=0, keepdims=True)
-        + steps * jnp.sum(shift * shift, axis=0, keepdims=True)
-    ) / total_steps
+    pl.semaphore_wait(barrier, Z + X + Y - 2)
+
+    def line(which, own, slots, count, me, device):
+        def copy(peer, slot):
+            return remote(own, slots.at[slot], line_s.at[which], line_r.at[which], device(peer))
+
+        rest = slots.at[pl.ds(0, count - 1)]
+        whole = remote(rest, rest, line_s.at[which], line_r.at[which], device(me))
+        for k in range(1, count):
+            copy(lax.rem(me + k, count), me).start()
+        slots[pl.ds(me, 1)] = own[...][None]
+        return whole
+
+    def combine(slots, count):
+        sums = slots[:, 0]
+        total = jnp.sum(sums, axis=0, keepdims=True)
+        shift = sums / count - total / (count * slots.shape[0])
+        squares = slots[:, 1] + count * (shift * shift)
+        return total, jnp.sum(squares, axis=0, keepdims=True)
+
+    line(0, stats, stats_z, Z, depth, on_z).wait()
+    total, squares = combine(stats_z, float(steps))
+    stats[0:1] = total
+    stats[1:2] = squares
+    line(1, stats, stats_x, X, across, on_x).wait()
+    total, squares = combine(stats_x, float(steps * Z))
+    mean = total / total_steps
+    variance = squares / total_steps
     inverse = lax.rsqrt(variance + epsilon)
     spread = jnp.sqrt(variance + epsilon)
+    for copy in params:
+        copy.wait()
     gain, offset = gain_ref[...], offset_ref[...]
     scale = spread / gain
 
@@ -358,75 +408,95 @@
 
     each(0, chunks, layer_two)
 
-    def one(g, src, dst, size, peer, slot):
+    groups = (
+        (early, early_pair, early_half, early_one, early_block, early_two, early_out, EARLY),
+        (late, late_pair, late_half, late_one, late_block, late_two, late_out, LATE),
+        (last, last_pair, last_half, last_one, last_block, last_two, last_out, LAST),
+    )
+
+    def pair(g):
+        src, got, size = groups[g][0], groups[g][1], groups[g][7] * PLANE
         return remote(
-            src.at[at(peer * size, size)],
-            dst.at[slot],
-            one_s.at[g, peer],
-            one_r.at[g, slot],
-            member(peer),
+            src.at[at((1 - core) * size, size)], got, pair_s.at[g], pair_r.at[g], mate
         )
 
-    def two(g, src, dst, peer, slot):
+    def one(g, k):
+        half, got, size = groups[g][2], groups[g][3], groups[g][7]
+        peer = lax.rem(mine + k, PLANE)
         return remote(
-            src, dst.at[slot], two_s.at[g, peer], two_r.at[g, slot], {"tm": place * Z + peer}
+            half.at[at(peer * size, size)], got.at[k], one_s.at[g], one_r.at[g], on_plane(peer)
         )
 
-    def three(g, out, size, peer, slot):
-        where = out.at[at(slot * size, size)]
-        return remote(where, where, three_s.at[g, peer], three_r.at[g, slot], member(peer))
-
-    groups = (
-        (early, early_one, early_block, early_two, early_out, EARLY),
-        (late, late_one, late_block, late_two, late_out, LATE),
-        (last, last_one, last_block, last_two, last_out, LAST),
-    )
+    def two(g, k):
+        block, got = groups[g][4], groups[g][5]
+        peer = lax.rem(depth + k, Z)
+        return remote(block, got.at[depth], two_s.at[g], two_r.at[g], on_z(peer))
+
+    def three(g, k):
+        out, size = groups[g][6], groups[g][7]
+        where = out.at[at((core * PLANE + mine) * size, size)]
+        peer = lax.rem(mine + k, PLANE)
+        return remote(where, where, three_s.at[g], three_r.at[g], on_plane(peer))
+
+    def back(g):
+        out, size = groups[g][6], groups[g][7] * PLANE
+        where = out.at[at(core * size, size)]
+        return remote(where, where, back_s.at[g], back_r.at[g], mate)
+
+    def whole(g, ref, count, s_sem, r_sem):
+        rest = ref.at[pl.ds(0, count)]
+        return remote(rest, rest, s_sem.at[g], r_sem.at[g], mate)
+
+    def all_one(g):
+        return whole(g, groups[g][3], PLANE - 1, one_s, one_r)
+
+    def all_two(g):
+        return whole(g, groups[g][5], Z - 1, two_s, two_r)
+
+    def all_three(g):
+        return whole(g, groups[g][6], (PLANE - 1) * groups[g][7], three_s, three_r)
+
+    def start(g):
+        pair(g).start()
 
     def scatter(g):
-        src, dst, block, _, _, size = groups[g]
-        each(1, GROUP, lambda k: one(g, src, dst, size, lax.rem(mine + k, GROUP), mine).start())
-        dst[pl.ds(mine, 1)] = src[at(mine * size, size)][None]
+        src, got, half, slots, _, _, _, size = groups[g]
+        pair(g).wait_recv()
+        half[...] = src[at(core * PLANE * size, PLANE * size)] + got[...]
+        each(1, PLANE, lambda k: one(g, k).start())
 
     def middle(g):
-        src, dst, block, far, _, size = groups[g]
-
-        def take(k):
-            peer = lax.rem(mine + k, GROUP)
-            one(g, src, dst, size, peer, peer).wait()
-
-        each(1, GROUP, take)
-        total = dst[0]
-        for p in range(1, GROUP):
-            total = total + dst[p]
+        _, _, half, slots, block, far, _, size = groups[g]
+        all_one(g).wait_recv()
+        total = half[at(mine * size, size)]
+        for p in range(1, PLANE):
+            total = total + slots[p]
         block[...] = total
-        each(1, Z, lambda k: two(g, block, far, lax.rem(depth + k, Z), depth).start())
+        each(1, Z, lambda k: two(g, k).start())
         far[pl.ds(depth, 1)] = total[None]
 
     def gather(g):
-        _, _, block, far, out, size = groups[g]
-
-        def take(k):
-            peer = lax.rem(depth + k, Z)
-            two(g, block, far, peer, peer).wait()
-
-        each(1, Z, take)
+        _, _, _, _, _, far, out, size = groups[g]
+        all_two(g).wait_recv()
         total = far[0]
         for z in range(1, Z):
             total = total + far[z]
-        out[at(mine * size, size)] = total
-        each(1, GROUP, lambda k: three(g, out, size, lax.rem(mine + k, GROUP), mine).start())
+        out[at((core * PLANE + mine) * size, size)] = total
+        each(1, PLANE, lambda k: three(g, k).start())
+
+    def share(g):
+        all_three(g).wait_recv()
+        back(g).start()
 
     def finish(g):
-        _, _, _, _, out, size = groups[g]
-
-        def take(k):
-            peer = lax.rem(mine + k, GROUP)
-            three(g, out, size, peer, mine).wait_send()
-            three(g, out, size, peer, peer).wait_recv()
-
-        each(1, GROUP, take)
-
-    scatter(0)
+        back(g).wait_recv()
+        pair(g).wait_send()
+        all_one(g).wait_send()
+        all_two(g).wait_send()
+        all_three(g).wait_send()
+        back(g).wait_send()
+
+    start(0)
 
     def back_one(c):
         @pl.when(jnp.logical_and(c == chunks - 1, tm < TM - 1))
@@ -454,8 +524,8 @@
             halo[3].start()
 
     each(0, chunks, back_one)
-    scatter(1)
-    middle(0)
+    start(1)
+    scatter(0)
 
     def back_zero(c):
         @pl.when(jnp.logical_and(c == chunks - 1, tm < TM - 1))
@@ -481,9 +551,8 @@
     ends[1:2] = sum_b
     ends[2:3] = out_a
     ends[3:4] = out_b
-    each(1, TM, lambda k: ends_copy(lax.rem(tm + k, TM), tm).start())
-    ends_all[pl.ds(tm, 1)] = ends[...][None]
-    for p in range(GROUP):
+    ends_line = line(2, ends, ends_z, Z, depth, on_z)
+    for p in range(PARTS):
         last[8 * p : 8 * p + 4] = in_grad[4 * p : 4 * p + 4]
     last[4:5] = (sum_b - out_b * spread) / gain
     last[12:13] = (sum_a - out_a * spread) / gain
@@ -491,33 +560,30 @@
     last[28:29] = column(7)
     last[36:37] = column(4)
     last[44:45] = column(5)
+    start(2)
+    scatter(1)
+    middle(0)
     scatter(2)
+    ends_line.wait()
+    ends[...] = jnp.sum(ends_z[...], axis=0)
+    ends_line = line(3, ends, ends_x, X, across, on_x)
+    middle(1)
     gather(0)
-    middle(1)
-
-    def take_ends(k):
-        peer = lax.rem(tm + k, TM)
-        ends_copy(peer, peer).wait()
-
-    each(1, TM, take_ends)
-    totals = jnp.sum(ends_all[...], axis=0) / total_steps
+    middle(2)
+    ends_line.wait()
+    totals = jnp.sum(ends_x[...], axis=0) / total_steps
     slant = inverse * (totals[3:4] - inverse * totals[1:2])
     level = totals[2:3] - inverse * totals[0:1]
-    middle(2)
-
-    def store(c):
-        return pltpu.make_async_copy(
-            hat.at[at(c * ROWS, ROWS)], grad_hbm.at[at(c * ROWS, ROWS)], store_sem.at[c]
-        )
-
     def resolve(c):
         now = at(c * ROWS, ROWS)
         hat[now] = hat[now] * inverse + ((x[now] - mean) * slant + level)
-        store(c).start()
 
     each(0, chunks, resolve)
     gather(1)
+    share(0)
     gather(2)
+    share(1)
+    share(2)
 
     @pl.when(tm < TM - 1)
     def _():
@@ -529,13 +595,16 @@
         halo[2].wait_send()
         halo[3].wait_send()
 
-    each(0, chunks, lambda c: store(c).wait())
     finish(0)
     finish(1)
     finish(2)
 
 
-def unpack_kernel(early, late, last, conv, bias, res, skip, out, into, gain, shift):
+def unpack_kernel(
+    hat, early, late, last, grad, conv, bias, res, skip, out, into, gain, shift, store_sem
+):
+    store = pltpu.make_async_copy(hat, grad, store_sem)
+    store.start()
     for layer, src in ((0, late), (1, early)):
         for tap in range(2):
             for half in range(2):
@@ -553,10 +622,11 @@
     out[0:128] = early[1024:1152]
     out[128:256] = late[640:768]
     res[...] = late[512:640]
-    for p in range(GROUP):
+    for p in range(PARTS):
         into[4 * p : 4 * p + 4] = last[8 * p : 8 * p + 4]
     gain[...] = last[4:5]
     shift[...] = last[12:13]
+    store.wait()
 
 
 def on_device(
@@ -574,26 +644,39 @@
     steps = series_data.shape[1]
     f32, bf16 = jnp.float32, jnp.bfloat16
     vmem = pl.BlockSpec(memory_space=pltpu.VMEM)
-    hbm = pl.BlockSpec(memory_space=pl.ANY)
+    hbm = pl.BlockSpec(memory_space=pltpu.HBM)
     sem = pltpu.SemaphoreType.DMA
     shape = jax.ShapeDtypeStruct
     field = pltpu.VMEM((steps, 128), f32)
 
-    def sizes(lead):
-        return [pltpu.VMEM((lead, size, 128), f32) for size in (EARLY, LATE, LAST)]
-
-    grad, early, late, last = pl.pallas_call(
+    sizes = (EARLY, LATE, LAST)
+
+    def slots(lead):
+        return [pltpu.VMEM((lead, size, 128), f32) for size in sizes]
+
+    def blocks(count):
+        return [pltpu.VMEM((count * size, 128), f32) for size in sizes]
+
+    hat, early, late, last = pl.pallas_call(
         block_kernel,
         name="block",
         out_shape=(
-            shape((steps, 128), f32),
-            shape((GROUP * EARLY, 128), f32),
-            shape((GROUP * LATE, 128), f32),
-            shape((GROUP * LAST, 128), f32),
+            pltpu.VMEM((steps, 128), f32),
+            pltpu.VMEM((PARTS * EARLY, 128), f32),
+            pltpu.VMEM((PARTS * LATE, 128), f32),
+            pltpu.VMEM((PARTS * LAST, 128), f32),
         ),
-        in_specs=[hbm, hbm] + [vmem] * 8,
-        out_specs=(hbm, vmem, vmem, vmem),
+        in_specs=[hbm] * 10,
+        out_specs=(vmem,) * 4,
         scratch_shapes=[
+            pltpu.VMEM((128, 128), bf16),
+            pltpu.VMEM((2, 256, 256), bf16),
+            pltpu.VMEM((2, 256), f32),
+            pltpu.VMEM((128, 128), bf16),
+            pltpu.VMEM((256, 256), bf16),
+            pltpu.VMEM((256, 128), bf16),
+            pltpu.VMEM((1, 128), f32),
+            pltpu.VMEM((1, 128), f32),
             field,
             field,
             pltpu.VMEM((steps + FIRST, 128), bf16),
@@ -606,38 +689,29 @@
             pltpu.VMEM((steps + SECOND, 128), f32),
             field,
             pltpu.VMEM((steps + FIRST, 128), f32),
-            field,
-            pltpu.VMEM((GROUP * EARLY, 128), f32),
-            pltpu.VMEM((GROUP * LATE, 128), f32),
-            pltpu.VMEM((GROUP * LAST, 128), f32),
+            *blocks(PARTS),
             pltpu.VMEM((128, 128), f32),
             pltpu.VMEM((10, 8, 128), f32),
             pltpu.VMEM((2, 128), f32),
-            pltpu.VMEM((TM, 2, 128), f32),
+            pltpu.VMEM((Z, 2, 128), f32),
+            pltpu.VMEM((X, 2, 128), f32),
             pltpu.VMEM((4, 128), f32),
-            pltpu.VMEM((TM, 4, 128), f32),
-            *sizes(GROUP),
-            *sizes(Z),
-            pltpu.VMEM((EARLY, 128), f32),
-            pltpu.VMEM((LATE, 128), f32),
-            pltpu.VMEM((LAST, 128), f32),
-            sem((steps // ROWS + 1,)),
-            sem((steps // ROWS,)),
+            pltpu.VMEM((Z, 4, 128), f32),
+            pltpu.VMEM((X, 4, 128), f32),
+            *blocks(PLANE),
+            *blocks(PLANE),
+            *slots(PLANE),
+            *slots(Z),
+            *blocks(1),
+            sem((steps // ROWS + 9,)),
             sem((4,)),
             sem((4,)),
-            sem((TM,)),
-            sem((TM,)),
-            sem((TM,)),
-            sem((TM,)),
-            sem((3, GROUP)),
-            sem((3, GROUP)),
-            sem((3, Z)),
-            sem((3, Z)),
-            sem((3, GROUP)),
-            sem((3, GROUP)),
+            sem((4,)),
+            sem((4,)),
+            *[sem((3,))] * 10,
         ],
         compiler_params=pltpu.CompilerParams(
-            collective_id=0, has_side_effects=True, vmem_limit_bytes=60 * 1024 * 1024
+            collective_id=0, has_side_effects=True, vmem_limit_bytes=56 * 1024 * 1024
         ),
     )(
         series_data[0],
@@ -651,10 +725,11 @@
         norm_gain_vector.reshape(1, 128),
         norm_offset_vector.reshape(1, 128),
     )
-    conv, bias, res, skip, out, into, gain, shift = pl.pallas_call(
+    grad, conv, bias, res, skip, out, into, gain, shift = pl.pallas_call(
         unpack_kernel,
         name="unpack",
         out_shape=(
+            shape((steps, 128), f32),
             shape((2, 2, 128, 256), f32),
             shape((2, 256), f32),
             shape((128, 128), f32),
@@ -664,9 +739,11 @@
             shape((1, 128), f32),
             shape((1, 128), f32),
         ),
-        in_specs=[vmem] * 3,
-        out_specs=(vmem,) * 8,
-    )(early, late, last)
+        in_specs=[vmem] * 4,
+        out_specs=(hbm,) + (vmem,) * 8,
+        scratch_shapes=[sem],
+        compiler_params=pltpu.CompilerParams(vmem_limit_bytes=8 * 1024 * 1024),
+    )(hat, early, late, last)
     return grad[None], conv, bias, res, skip, out, into, gain.reshape(128), shift.reshape(128)
 
 

time: 81.3 us -> 67.3 us (0.83)
  Pallas kernels: 77.5 us -> 66.6 us
  local copies, waits for them, and re-layouts: 3.05 us -> 0 us
    pallas_call x2, Pallas kernels: 77.5 us -> 66.6 us  [the longest x1 64.3 us: on_device(): pl.pallas_call(block_kernel, name='block', out_shape=(pltpu.VMEM((steps,...]
    unnamed x1 -> x0, local copies, waits for them, and re-layouts: 3.05 us -> none
where the time goes in v3:
time: 67.3 us; the launch traced here: 67.2 us
  Pallas kernels  66.6 us (99%)
    pallas_call x1, Pallas kernels, on_device(): pl.pallas_call(block_kernel, name='block', out_shape=(pltpu.VMEM((steps,...  64.3 us
    pallas_call x1, Pallas kernels, on_device(): pl.pallas_call(unpack_kernel, name='unpack', out_shape=(shape((steps, 128...  2.3 us

profile of v3, /device:TPU:1, one launch (start us, length us, event | category | flops | bytes accessed | tf_op | source)
XLA Modules:
  0.0 67.2 jit_solution(6173928415443707854)
XLA Ops:
  0.6 64.3 %block.1 = (f32[4096,128]{1,0:T(8,128)S(1)}, f32[1280,128]{1,0:T(8,128)S(1)}, f32[768,128]{1,0:T(8,128)S(1)}, f32[256,128]{1,0:T(8,128)S(1)}) custom-call(f32[4096,128]{1,0:T(8,128)} %bitcast.9, f32[4096,128]{1,0:T(8,128)} %bitcast.10, bf16[128,128]{1,0:T(8,128)(2,1)} %w_in_hbm.1, bf16[2,256,256]{2,1,0:T(8,128)(2,1)} %bitcast.11, f32[2,256]{1,0:T(2,128)} %bias_hbm.1, ...), custom_call_target="tpu_custom_call" | custom-call | tf_op jit(solution)/shard_map/block/pallas_call | solution.py:660
  64.9 2.3 %unpack.1 = (f32[4096,128]{1,0:T(8,128)}, f32[2,2,128,256]{3,2,1,0:T(8,128)}, f32[2,256]{1,0:T(2,128)}, f32[128,128]{1,0:T(8,128)}, f32[2,128,256]{2,1,0:T(8,128...) custom-call(f32[4096,128]{1,0:T(8,128)S(1)} %get-tuple-element.22.hat, ...), custom_call_target="tpu_custom_call" | custom-call | tf_op jit(solution)/shard_map/unpack/pallas_call | solution.py:728

commit v4 on v3

--- a/solution.py
+++ b/solution.py
@@ -14,9 +14,9 @@
 Y = 4
 PLANE = X * Y
 PARTS = 2 * PLANE
-ROWS = 512
+ROWS = 2048
 MESH = pl.DeviceIdType.MESH
-EARLY, LATE, LAST = 40, 24, 8
+EARLY, LATE, LAST = 32, 32, 8
 
 epsilon = 1e-05
 gelu_coeff = 0.7978845608
@@ -118,6 +118,9 @@
     early_half,
     late_half,
     last_half,
+    early_send,
+    late_send,
+    last_send,
     early_one,
     late_one,
     last_one,
@@ -383,8 +386,7 @@
         acc[3] += fold(gradient * (forecast - offset))
         scaled = (gradient * scale).astype(jnp.bfloat16)
         out_part = tn(rectified, scaled)
-        early[1024:1152] += out_part[:128]
-        late[640:768] += out_part[128:]
+        late[640:896] += out_part
         back_skip = (nt(scaled, w_out[...]) * slope).astype(jnp.bfloat16)
         skip_part = tn(both, back_skip)
         early[512:768] += skip_part[:, :128]
@@ -413,18 +415,20 @@
         (late, late_pair, late_half, late_one, late_block, late_two, late_out, LATE),
         (last, last_pair, last_half, last_one, last_block, last_two, last_out, LAST),
     )
+    sends = (early_send, late_send, last_send)
 
     def pair(g):
-        src, got, size = groups[g][0], groups[g][1], groups[g][7] * PLANE
-        return remote(
-            src.at[at((1 - core) * size, size)], got, pair_s.at[g], pair_r.at[g], mate
-        )
+        return remote(sends[g], groups[g][1], pair_s.at[g], pair_r.at[g], mate)
 
     def one(g, k):
-        half, got, size = groups[g][2], groups[g][3], groups[g][7]
+        got, size = groups[g][3], groups[g][7]
         peer = lax.rem(mine + k, PLANE)
         return remote(
-            half.at[at(peer * size, size)], got.at[k], one_s.at[g], one_r.at[g], on_plane(peer)
+            sends[g].at[at(peer * size, size)],
+            got.at[k],
+            one_s.at[g],
+            one_r.at[g],
+            on_plane(peer),
         )
 
     def two(g, k):
@@ -456,13 +460,20 @@
     def all_three(g):
         return whole(g, groups[g][6], (PLANE - 1) * groups[g][7], three_s, three_r)
 
+    def wide(values):
+        return values.astype(jnp.float32)
+
     def start(g):
+        src, size = groups[g][0], groups[g][7] * PLANE
+        sends[g][...] = src[at((1 - core) * size, size)].astype(sends[g].dtype)
         pair(g).start()
 
     def scatter(g):
         src, got, half, slots, _, _, _, size = groups[g]
-        pair(g).wait_recv()
-        half[...] = src[at(core * PLANE * size, PLANE * size)] + got[...]
+        pair(g).wait()
+        total = src[at(core * PLANE * size, PLANE * size)] + wide(got[...])
+        half[...] = total
+        sends[g][...] = total.astype(sends[g].dtype)
         each(1, PLANE, lambda k: one(g, k).start())
 
     def middle(g):
@@ -470,18 +481,18 @@
         all_one(g).wait_recv()
         total = half[at(mine * size, size)]
         for p in range(1, PLANE):
-            total = total + slots[p]
-        block[...] = total
+            total = total + wide(slots[p])
+        block[...] = total.astype(block.dtype)
         each(1, Z, lambda k: two(g, k).start())
-        far[pl.ds(depth, 1)] = total[None]
+        far[pl.ds(depth, 1)] = block[...][None]
 
     def gather(g):
         _, _, _, _, _, far, out, size = groups[g]
         all_two(g).wait_recv()
-        total = far[0]
+        total = wide(far[0])
         for z in range(1, Z):
-            total = total + far[z]
-        out[at((core * PLANE + mine) * size, size)] = total
+            total = total + wide(far[z])
+        out[at((core * PLANE + mine) * size, size)] = total.astype(out.dtype)
         each(1, PLANE, lambda k: three(g, k).start())
 
     def share(g):
@@ -490,7 +501,6 @@
 
     def finish(g):
         back(g).wait_recv()
-        pair(g).wait_send()
         all_one(g).wait_send()
         all_two(g).wait_send()
         all_three(g).wait_send()
@@ -502,6 +512,10 @@
         @pl.when(jnp.logical_and(c == chunks - 1, tm < TM - 1))
         def _():
             halo[2].wait_recv()
+
+        @pl.when(c == chunks - 1)
+        def _():
+            scatter(0)
 
         now = at(c * ROWS, ROWS)
         arrived = near_one[now] + far_one[at(c * ROWS + SECOND, ROWS)]
@@ -525,12 +539,15 @@
 
     each(0, chunks, back_one)
     start(1)
-    scatter(0)
 
     def back_zero(c):
         @pl.when(jnp.logical_and(c == chunks - 1, tm < TM - 1))
         def _():
             halo[3].wait_recv()
+
+        @pl.when(c == chunks - 1)
+        def _():
+            scatter(1)
 
         now = at(c * ROWS, ROWS)
         grad_zero = (near_zero[now] + far_zero[at(c * ROWS + FIRST, ROWS)]).astype(jnp.bfloat16)
@@ -561,15 +578,14 @@
     last[36:37] = column(4)
     last[44:45] = column(5)
     start(2)
-    scatter(1)
+    scatter(2)
     middle(0)
-    scatter(2)
     ends_line.wait()
     ends[...] = jnp.sum(ends_z[...], axis=0)
     ends_line = line(3, ends, ends_x, X, across, on_x)
     middle(1)
+    middle(2)
     gather(0)
-    middle(2)
     ends_line.wait()
     totals = jnp.sum(ends_x[...], axis=0) / total_steps
     slant = inverse * (totals[3:4] - inverse * totals[1:2])
@@ -610,18 +626,17 @@
             for half in range(2):
                 conv[layer, tap, :, half * 128 : half * 128 + 128] = src[
                     pl.ds(half * 256 + tap * 128, 128)
-                ]
+                ].astype(jnp.float32)
     for layer in range(2):
         for half in range(2):
             skip[layer, :, half * 128 : half * 128 + 128] = early[
                 pl.ds(512 + half * 256 + layer * 128, 128)
-            ]
+            ].astype(jnp.float32)
             bias[layer : layer + 1, half * 128 : half * 128 + 128] = last[
                 pl.ds(20 + layer * 16 + half * 8, 1)
             ]
-    out[0:128] = early[1024:1152]
-    out[128:256] = late[640:768]
-    res[...] = late[512:640]
+    out[...] = late[640:896].astype(jnp.float32)
+    res[...] = late[512:640].astype(jnp.float32)
     for p in range(PARTS):
         into[4 * p : 4 * p + 4] = last[8 * p : 8 * p + 4]
     gain[...] = last[4:5]
@@ -650,21 +665,23 @@
     field = pltpu.VMEM((steps, 128), f32)
 
     sizes = (EARLY, LATE, LAST)
+    wires = (bf16, bf16, f32)
 
     def slots(lead):
-        return [pltpu.VMEM((lead, size, 128), f32) for size in sizes]
+        return [pltpu.VMEM((lead, n, 128), wire) for n, wire in zip(sizes, wires)]
 
     def blocks(count):
-        return [pltpu.VMEM((count * size, 128), f32) for size in sizes]
+        return [pltpu.VMEM((count * n, 128), wire) for n, wire in zip(sizes, wires)]
+
+    def wide_blocks(count):
+        return [pltpu.VMEM((count * n, 128), f32) for n in sizes]
 
     hat, early, late, last = pl.pallas_call(
         block_kernel,
         name="block",
         out_shape=(
             pltpu.VMEM((steps, 128), f32),
-            pltpu.VMEM((PARTS * EARLY, 128), f32),
-            pltpu.VMEM((PARTS * LATE, 128), f32),
-            pltpu.VMEM((PARTS * LAST, 128), f32),
+            *blocks(PARTS),
         ),
         in_specs=[hbm] * 10,
         out_specs=(vmem,) * 4,
@@ -689,7 +706,7 @@
             pltpu.VMEM((steps + SECOND, 128), f32),
             field,
             pltpu.VMEM((steps + FIRST, 128), f32),
-            *blocks(PARTS),
+            *wide_blocks(PARTS),
             pltpu.VMEM((128, 128), f32),
             pltpu.VMEM((10, 8, 128), f32),
             pltpu.VMEM((2, 128), f32),
@@ -699,6 +716,7 @@
             pltpu.VMEM((Z, 4, 128), f32),
             pltpu.VMEM((X, 4, 128), f32),
             *blocks(PLANE),
+            *wide_blocks(PLANE),
             *blocks(PLANE),
             *slots(PLANE),
             *slots(Z),

time: 67.3 us -> 59.7 us (0.89)
  Pallas kernels: 66.6 us -> 59 us
    pallas_call x1, Pallas kernels: 64.3 us -> 56.7 us  [on_device(): pl.pallas_call(block_kernel, name='block', out_shape=(pltpu.VMEM((steps,...]
where the time goes in v4:
time: 59.7 us; the launch traced here: 59.6 us
  Pallas kernels  59 us (99%)
  between operations  0.65 us (1%)
    pallas_call x1, Pallas kernels, on_device(): pl.pallas_call(block_kernel, name='block', out_shape=(pltpu.VMEM((steps,...  56.7 us
    pallas_call x1, Pallas kernels, on_device(): pl.pallas_call(unpack_kernel, name='unpack', out_shape=(shape((steps, 128...  2.3 us

profile of v4, /device:TPU:1, one launch (start us, length us, event | category | flops | bytes accessed | tf_op | source)
XLA Modules:
  0.0 59.6 jit_solution(16802542925019156038)
XLA Ops:
  0.6 56.7 %block.1 = (f32[4096,128]{1,0:T(8,128)S(1)}, bf16[1024,128]{1,0:T(8,128)(2,1)S(1)}, bf16[1024,128]{1,0:T(8,128)(2,1)S(1)}, f32[256,128]{1,0:T(8,128)S(1)}) custom-call(f32[4096,128]{1,0:T(8,128)} %bitcast.9, f32[4096,128]{1,0:T(8,128)} %bitcast.10, bf16[128,128]{1,0:T(8,128)(2,1)} %w_in_hbm.1, bf16[2,256,256]{2,1,0:T(8,128)(2,1)} %bitcast.11, ...), custom_call_target="tpu_custom_call" | custom-call | tf_op jit(solution)/shard_map/block/pallas_call | solution.py:679
  57.3 2.3 %unpack.1 = (f32[4096,128]{1,0:T(8,128)}, f32[2,2,128,256]{3,2,1,0:T(8,128)}, f32[2,256]{1,0:T(2,128)}, f32[128,128]{1,0:T(8,128)}, f32[2,128,256]{2,1,0:T(8,128...) custom-call(f32[4096,128]{1,0:T(8,128)S(1)} %get-tuple-element.22.hat, ...), custom_call_target="tpu_custom_call" | custom-call | tf_op jit(solution)/shard_map/unpack/pallas_call | solution.py:746

commit v5 on v4

--- a/solution.py
+++ b/solution.py
@@ -14,7 +14,7 @@
 Y = 4
 PLANE = X * Y
 PARTS = 2 * PLANE
-ROWS = 2048
+ROWS = 1024
 MESH = pl.DeviceIdType.MESH
 EARLY, LATE, LAST = 32, 32, 8
 
@@ -101,6 +101,10 @@
     far_one,
     near_zero,
     far_zero,
+    far_one_head,
+    far_one_tail,
+    far_zero_head,
+    far_zero_tail,
     early,
     late,
     last,
@@ -114,13 +118,10 @@
     ends_x,
     early_pair,
     late_pair,
-    last_pair,
     early_half,
     late_half,
-    last_half,
     early_send,
     late_send,
-    last_send,
     early_one,
     late_one,
     last_one,
@@ -217,8 +218,8 @@
 
     @pl.when(tm == TM - 1)
     def _():
-        far_one[pl.ds(steps, SECOND)] = jnp.zeros((SECOND, 128), jnp.float32)
-        far_zero[pl.ds(steps, FIRST)] = jnp.zeros((FIRST, 128), jnp.float32)
+        far_one_tail[...] = jnp.zeros_like(far_one_tail)
+        far_zero_tail[...] = jnp.zeros_like(far_zero_tail)
 
     def sum_x(c):
         load_x(c).wait()
@@ -287,72 +288,64 @@
             later,
         ),
         remote(
-            far_one.at[pl.ds(0, SECOND)],
-            far_one.at[pl.ds(steps, SECOND)],
+            far_one_head,
+            far_one_tail,
             halo_s.at[2],
             halo_r.at[2],
             earlier,
         ),
         remote(
-            far_zero.at[pl.ds(0, FIRST)],
-            far_zero.at[pl.ds(steps, FIRST)],
+            far_zero_head,
+            far_zero_tail,
             halo_s.at[3],
             halo_r.at[3],
             earlier,
         ),
     )
 
-    def normalize(c):
-        hat_x = (x[at(c * ROWS, ROWS)] - mean) * inverse
+    has_later, has_earlier = tm < TM - 1, tm > 0
+
+    def normalize(start, size):
+        hat_x = (x[pl.ds(start, size)] - mean) * inverse
         return hat_x, (hat_x * gain + offset).astype(jnp.bfloat16)
 
-    def project(i):
-        c = chunks - 1 - i
-        _, normed = normalize(c)
-        level_zero[at(FIRST + c * ROWS, ROWS)] = nn(normed, w_in[...]).astype(jnp.bfloat16)
-
-        @pl.when(jnp.logical_and(i == 0, tm < TM - 1))
-        def _():
-            halo[0].start()
-
-    each(0, chunks, project)
+    def project(start, size):
+        _, normed = normalize(start, size)
+        level_zero[pl.ds(FIRST + start, size)] = nn(normed, w_in[...]).astype(jnp.bfloat16)
 
     def gates(act):
         return jnp.tanh(act[:, :128]), 0.5 * jnp.tanh(0.5 * act[:, 128:]) + 0.5
 
-    def window_zero(c):
+    def window_zero(start, size):
         return jnp.concatenate(
-            [level_zero[at(c * ROWS, ROWS)], level_zero[at(c * ROWS + FIRST, ROWS)]], axis=1
+            [level_zero[pl.ds(start, size)], level_zero[pl.ds(start + FIRST, size)]], axis=1
         )
 
-    def window_one(c):
+    def window_one(start, size):
         return jnp.concatenate(
-            [level_one[at(c * ROWS, ROWS)], level_one[at(c * ROWS + SECOND, ROWS)]], axis=1
+            [level_one[pl.ds(start, size)], level_one[pl.ds(start + SECOND, size)]], axis=1
         )
 
-    def layer_one(i):
-        c = chunks - 1 - i
-
-        @pl.when(jnp.logical_and(c == 0, tm > 0))
-        def _():
-            halo[0].wait_recv()
-
-        now = at(c * ROWS, ROWS)
-        tanh, sigm = gates(nn(window_zero(c), w_conv[0]) + bias[0:1])
+    def layer_one(start, size):
+        now = pl.ds(start, size)
+        tanh, sigm = gates(nn(window_zero(start, size), w_conv[0]) + bias[0:1])
         gated = (tanh * sigm).astype(jnp.bfloat16)
         tanh_one[now] = tanh
         sigm_one[now] = sigm
         gated_one[now] = gated
-        level = level_zero[at(c * ROWS + FIRST, ROWS)].astype(jnp.float32)
-        level_one[at(c * ROWS + SECOND, ROWS)] = (level + nn(gated, w_res[...])).astype(
+        level = level_zero[pl.ds(start + FIRST, size)].astype(jnp.float32)
+        level_one[pl.ds(start + SECOND, size)] = (level + nn(gated, w_res[...])).astype(
             jnp.bfloat16
         )
 
-        @pl.when(jnp.logical_and(i == 0, tm < TM - 1))
-        def _():
-            halo[1].start()
-
-    each(0, chunks, layer_one)
+    project(steps - SECOND - FIRST, SECOND + FIRST)
+    pl.when(has_later)(halo[0].start)
+    layer_one(steps - SECOND, SECOND)
+    pl.when(has_later)(halo[1].start)
+    project(0, steps - SECOND - FIRST)
+    layer_one(SECOND, steps - 2 * SECOND)
+    pl.when(has_earlier)(halo[0].wait_recv)
+    layer_one(0, SECOND)
 
     def gate_back(incoming, tanh, sigm):
         part = incoming * sigm
@@ -360,13 +353,9 @@
 
     load_cot.wait()
 
-    @pl.when(tm > 0)
-    def _():
-        halo[1].wait_recv()
-
-    def layer_two(c):
-        now = at(c * ROWS, ROWS)
-        window = window_one(c)
+    def layer_two(start, size):
+        now = pl.ds(start, size)
+        window = window_one(start, size)
         tanh, sigm = gates(nn(window, w_conv[1]) + bias[1:2])
         gated = (tanh * sigm).astype(jnp.bfloat16)
         both = jnp.concatenate([gated_one[now], gated], axis=1)
@@ -404,18 +393,19 @@
         far_one[now] = carried[:, :128]
         near_one[now] = carried[:, 128:]
 
-        @pl.when(jnp.logical_and(c == 0, tm > 0))
-        def _():
-            halo[2].start()
-
-    each(0, chunks, layer_two)
+    layer_two(5 * SECOND, steps - 5 * SECOND)
+    pl.when(has_earlier)(halo[1].wait_recv)
+    layer_two(0, SECOND)
+    far_one_head[...] = far_one[pl.ds(0, SECOND)].astype(jnp.bfloat16)
+    pl.when(has_earlier)(halo[2].start)
+    layer_two(SECOND, 4 * SECOND)
 
     groups = (
         (early, early_pair, early_half, early_one, early_block, early_two, early_out, EARLY),
         (late, late_pair, late_half, late_one, late_block, late_two, late_out, LATE),
-        (last, last_pair, last_half, last_one, last_block, last_two, last_out, LAST),
+        (last, None, None, last_one, last_block, last_two, last_out, LAST),
     )
-    sends = (early_send, late_send, last_send)
+    sends = (early_send, late_send)
 
     def pair(g):
         return remote(sends[g], groups[g][1], pair_s.at[g], pair_r.at[g], mate)
@@ -438,7 +428,7 @@
 
     def three(g, k):
         out, size = groups[g][6], groups[g][7]
-        where = out.at[at((core * PLANE + mine) * size, size)]
+        where = out.at[at(owner * size, size)]
         peer = lax.rem(mine + k, PLANE)
         return remote(where, where, three_s.at[g], three_r.at[g], on_plane(peer))
 
@@ -451,14 +441,35 @@
         rest = ref.at[pl.ds(0, count)]
         return remote(rest, rest, s_sem.at[g], r_sem.at[g], mate)
 
+    owner = core * PLANE + mine
+
+    def on_owner(p):
+        member = lax.rem(p, PLANE)
+        return {
+            "series": lax.rem(member, Y) * 2 + p // PLANE,
+            "tm": (member // Y) * Z + depth,
+        }
+
+    def last_one_copy(k):
+        peer = lax.rem(owner + k, PARTS)
+        return remote(
+            last.at[at(peer * LAST, LAST)], last_one.at[k], one_s.at[2], one_r.at[2], on_owner(peer)
+        )
+
+    def last_three_copy(k):
+        where = last_out.at[at(owner * LAST, LAST)]
+        peer = lax.rem(owner + k, PARTS)
+        return remote(where, where, three_s.at[2], three_r.at[2], on_owner(peer))
+
     def all_one(g):
-        return whole(g, groups[g][3], PLANE - 1, one_s, one_r)
+        return whole(g, groups[g][3], groups[g][3].shape[0] - 1, one_s, one_r)
 
     def all_two(g):
         return whole(g, groups[g][5], Z - 1, two_s, two_r)
 
     def all_three(g):
-        return whole(g, groups[g][6], (PLANE - 1) * groups[g][7], three_s, three_r)
+        peers = (PARTS if g == 2 else PLANE) - 1
+        return whole(g, groups[g][6], peers * groups[g][7], three_s, three_r)
 
     def wide(values):
         return values.astype(jnp.float32)
@@ -479,8 +490,8 @@
     def middle(g):
         _, _, half, slots, block, far, _, size = groups[g]
         all_one(g).wait_recv()
-        total = half[at(mine * size, size)]
-        for p in range(1, PLANE):
+        total = last[at(owner * size, size)] if g == 2 else half[at(mine * size, size)]
+        for p in range(1, slots.shape[0]):
             total = total + wide(slots[p])
         block[...] = total.astype(block.dtype)
         each(1, Z, lambda k: two(g, k).start())
@@ -492,73 +503,73 @@
         total = wide(far[0])
         for z in range(1, Z):
             total = total + wide(far[z])
-        out[at((core * PLANE + mine) * size, size)] = total.astype(out.dtype)
-        each(1, PLANE, lambda k: three(g, k).start())
+        out[at(owner * size, size)] = total.astype(out.dtype)
+        if g == 2:
+            each(1, PARTS, lambda k: last_three_copy(k).start())
+        else:
+            each(1, PLANE, lambda k: three(g, k).start())
 
     def share(g):
         all_three(g).wait_recv()
-        back(g).start()
+        if g < 2:
+            back(g).start()
 
     def finish(g):
-        back(g).wait_recv()
+        if g < 2:
+            back(g).wait()
         all_one(g).wait_send()
         all_two(g).wait_send()
         all_three(g).wait_send()
-        back(g).wait_send()
 
     start(0)
 
-    def back_one(c):
-        @pl.when(jnp.logical_and(c == chunks - 1, tm < TM - 1))
-        def _():
-            halo[2].wait_recv()
-
-        @pl.when(c == chunks - 1)
-        def _():
-            scatter(0)
-
-        now = at(c * ROWS, ROWS)
-        arrived = near_one[now] + far_one[at(c * ROWS + SECOND, ROWS)]
-        grad_one = arrived.astype(jnp.bfloat16)
+    def back_one(start, size):
+        now = pl.ds(start, size)
+        last_rows = start + size == steps
+        far = wide(far_one_tail[...]) if last_rows else far_one[pl.ds(start + SECOND, size)]
+        grad_one = (near_one[now] + far).astype(jnp.bfloat16)
         late[512:640] += tn(gated_one[now], grad_one)
         incoming = incoming_one[now] + nt(grad_one, w_res[...])
         first, second = gate_back(incoming, tanh_one[now], sigm_one[now])
         acc[6] += fold(first)
         acc[7] += fold(second)
         pre = jnp.concatenate([first, second], axis=1).astype(jnp.bfloat16)
-        conv_part = tn(window_zero(c), pre)
+        conv_part = tn(window_zero(start, size), pre)
         late[0:256] += conv_part[:, :128]
         late[256:512] += conv_part[:, 128:]
         carried = nt(pre, w_conv[0])
         far_zero[now] = carried[:, :128]
         near_zero[now] = grad_one.astype(jnp.float32) + carried[:, 128:]
 
-        @pl.when(jnp.logical_and(c == 0, tm > 0))
-        def _():
-            halo[3].start()
-
-    each(0, chunks, back_one)
+    back_one(0, SECOND)
+    far_zero_head[...] = far_zero[pl.ds(0, FIRST)].astype(jnp.bfloat16)
+    pl.when(has_earlier)(halo[3].start)
+    scatter(0)
+    back_one(SECOND, steps - 2 * SECOND)
+    pl.when(has_later)(halo[2].wait_recv)
+    back_one(steps - SECOND, SECOND)
     start(1)
 
-    def back_zero(c):
-        @pl.when(jnp.logical_and(c == chunks - 1, tm < TM - 1))
-        def _():
-            halo[3].wait_recv()
-
-        @pl.when(c == chunks - 1)
-        def _():
-            scatter(1)
-
-        now = at(c * ROWS, ROWS)
-        grad_zero = (near_zero[now] + far_zero[at(c * ROWS + FIRST, ROWS)]).astype(jnp.bfloat16)
-        hat_x, normed = normalize(c)
+    def back_zero(start, size):
+        now = pl.ds(start, size)
+        if start + size == steps:
+            far = jnp.concatenate(
+                [far_zero[pl.ds(start + FIRST, size - FIRST)], wide(far_zero_tail[...])], axis=0
+            )
+        else:
+            far = far_zero[pl.ds(start + FIRST, size)]
+        grad_zero = (near_zero[now] + far).astype(jnp.bfloat16)
+        hat_x, normed = normalize(start, size)
         in_grad[...] += tn(normed, grad_zero)
         grad_hat = nt(grad_zero, w_in[...]) * gain
         hat[now] = grad_hat
         acc[8] += fold(grad_hat)
         acc[9] += fold(grad_hat * hat_x)
 
-    each(0, chunks, back_zero)
+    back_zero(0, steps - SECOND)
+    pl.when(has_later)(halo[3].wait_recv)
+    scatter(1)
+    back_zero(steps - SECOND, SECOND)
 
     def column(k):
         return jnp.sum(acc[k], axis=0, keepdims=True)
@@ -577,8 +588,7 @@
     last[28:29] = column(7)
     last[36:37] = column(4)
     last[44:45] = column(5)
-    start(2)
-    scatter(2)
+    each(1, PARTS, lambda k: last_one_copy(k).start())
     middle(0)
     ends_line.wait()
     ends[...] = jnp.sum(ends_z[...], axis=0)
@@ -703,9 +713,13 @@
             field,
             field,
             field,
-            pltpu.VMEM((steps + SECOND, 128), f32),
-            field,
-            pltpu.VMEM((steps + FIRST, 128), f32),
+            field,
+            field,
+            field,
+            pltpu.VMEM((SECOND, 128), bf16),
+            pltpu.VMEM((SECOND, 128), bf16),
+            pltpu.VMEM((FIRST, 128), bf16),
+            pltpu.VMEM((FIRST, 128), bf16),
             *wide_blocks(PARTS),
             pltpu.VMEM((128, 128), f32),
             pltpu.VMEM((10, 8, 128), f32),
@@ -715,10 +729,11 @@
             pltpu.VMEM((4, 128), f32),
             pltpu.VMEM((Z, 4, 128), f32),
             pltpu.VMEM((X, 4, 128), f32),
-            *blocks(PLANE),
-            *wide_blocks(PLANE),
-            *blocks(PLANE),
-            *slots(PLANE),
+            *blocks(PLANE)[:2],
+            *wide_blocks(PLANE)[:2],
+            *blocks(PLANE)[:2],
+            *slots(PLANE)[:2],
+            pltpu.VMEM((PARTS, LAST, 128), f32),
             *slots(Z),
             *blocks(1),
             sem((steps // ROWS + 9,)),

time: 59.7 us -> 57.2 us (0.958)
  Pallas kernels: 59 us -> 56.3 us
    pallas_call x1, Pallas kernels: 56.7 us -> 54 us  [on_device(): pl.pallas_call(block_kernel, name='block', out_shape=(pltpu.VMEM((steps,...]
where the time goes in v5:
time: 57.2 us; the launch traced here: 57.1 us
  Pallas kernels  56.3 us (98%)
  between operations  0.81 us (1%)
    pallas_call x1, Pallas kernels, on_device(): pl.pallas_call(block_kernel, name='block', out_shape=(pltpu.VMEM((steps,...  54 us
    pallas_call x1, Pallas kernels, on_device(): pl.pallas_call(unpack_kernel, name='unpack', out_shape=(shape((steps, 128...  2.3 us

profile of v5, /device:TPU:1, one launch (start us, length us, event | category | flops | bytes accessed | tf_op | source)
XLA Modules:
  0.0 57.1 jit_solution(262300838194214683)
XLA Ops:
  0.6 54.0 %block.1 = (f32[4096,128]{1,0:T(8,128)S(1)}, bf16[1024,128]{1,0:T(8,128)(2,1)S(1)}, bf16[1024,128]{1,0:T(8,128)(2,1)S(1)}, f32[256,128]{1,0:T(8,128)S(1)}) custom-call(f32[4096,128]{1,0:T(8,128)} %bitcast.9, f32[4096,128]{1,0:T(8,128)} %bitcast.10, bf16[128,128]{1,0:T(8,128)(2,1)} %w_in_hbm.1, bf16[2,256,256]{2,1,0:T(8,128)(2,1)} %bitcast.11, ...), custom_call_target="tpu_custom_call" | custom-call | tf_op jit(solution)/shard_map/block/pallas_call | solution.py:689
  54.7 2.3 %unpack.1 = (f32[4096,128]{1,0:T(8,128)}, f32[2,2,128,256]{3,2,1,0:T(8,128)}, f32[2,256]{1,0:T(2,128)}, f32[128,128]{1,0:T(8,128)}, f32[2,128,256]{2,1,0:T(8,128...) custom-call(f32[4096,128]{1,0:T(8,128)S(1)} %get-tuple-element.22.hat, ...), custom_call_target="tpu_custom_call" | custom-call | tf_op jit(solution)/shard_map/unpack/pallas_call | solution.py:761

commit v6 on v5

--- a/solution.py
+++ b/solution.py
@@ -110,9 +110,9 @@
     last,
     in_grad,
     acc,
+    pieces,
     stats,
-    stats_z,
-    stats_x,
+    stats_all,
     ends,
     ends_z,
     ends_x,
@@ -197,10 +197,8 @@
     def hello(device):
         pl.semaphore_signal(barrier, inc=1, device_id=device, device_id_type=MESH)
 
-    for k in range(1, Z):
-        hello(on_z(lax.rem(depth + k, Z)))
-    for k in range(1, X):
-        hello(on_x(lax.rem(across + k, X)))
+    for k in range(1, TM):
+        hello({"tm": lax.rem(tm + k, TM)})
     for k in range(1, Y):
         hello({"series": lax.rem(up + k, Y) * 2 + core})
     hello(mate)
@@ -221,22 +219,27 @@
         far_one_tail[...] = jnp.zeros_like(far_one_tail)
         far_zero_tail[...] = jnp.zeros_like(far_zero_tail)
 
+    def combine(slots, count):
+        sums = slots[:, 0]
+        total = jnp.sum(sums, axis=0, keepdims=True)
+        shift = sums / count - total / (count * slots.shape[0])
+        squares = slots[:, 1] + count * (shift * shift)
+        return total, jnp.sum(squares, axis=0, keepdims=True)
+
     def sum_x(c):
         load_x(c).wait()
-        acc[0] += fold(x[at(c * ROWS, ROWS)])
+        values = x[at(c * ROWS, ROWS)]
+        total = jnp.sum(fold(values), axis=0, keepdims=True)
+        centred = values - total / ROWS
+        squares = jnp.sum(fold(centred * centred), axis=0, keepdims=True)
+        pieces[pl.ds(c, 1), 0:1] = total[None]
+        pieces[pl.ds(c, 1), 1:2] = squares[None]
 
     each(0, chunks, sum_x)
-    local_sum = jnp.sum(acc[0], axis=0, keepdims=True)
-    local_mean = local_sum / steps
-
-    def sum_squares(c):
-        centred = x[at(c * ROWS, ROWS)] - local_mean
-        acc[1] += fold(centred * centred)
-
-    each(0, chunks, sum_squares)
-    stats[0:1] = local_sum
-    stats[1:2] = jnp.sum(acc[1], axis=0, keepdims=True)
-    pl.semaphore_wait(barrier, Z + X + Y - 2)
+    total, squares = combine(pieces, float(ROWS))
+    stats[0:1] = total
+    stats[1:2] = squares
+    pl.semaphore_wait(barrier, TM + Y - 1)
 
     def line(which, own, slots, count, me, device):
         def copy(peer, slot):
@@ -249,19 +252,8 @@
         slots[pl.ds(me, 1)] = own[...][None]
         return whole
 
-    def combine(slots, count):
-        sums = slots[:, 0]
-        total = jnp.sum(sums, axis=0, keepdims=True)
-        shift = sums / count - total / (count * slots.shape[0])
-        squares = slots[:, 1] + count * (shift * shift)
-        return total, jnp.sum(squares, axis=0, keepdims=True)
-
-    line(0, stats, stats_z, Z, depth, on_z).wait()
-    total, squares = combine(stats_z, float(steps))
-    stats[0:1] = total
-    stats[1:2] = squares
-    line(1, stats, stats_x, X, across, on_x).wait()
-    total, squares = combine(stats_x, float(steps * Z))
+    line(0, stats, stats_all, TM, tm, lambda peer: {"tm": peer}).wait()
+    total, squares = combine(stats_all, float(steps))
     mean = total / total_steps
     variance = squares / total_steps
     inverse = lax.rsqrt(variance + epsilon)
@@ -344,8 +336,6 @@
     pl.when(has_later)(halo[1].start)
     project(0, steps - SECOND - FIRST)
     layer_one(SECOND, steps - 2 * SECOND)
-    pl.when(has_earlier)(halo[0].wait_recv)
-    layer_one(0, SECOND)
 
     def gate_back(incoming, tanh, sigm):
         part = incoming * sigm
@@ -394,6 +384,8 @@
         near_one[now] = carried[:, 128:]
 
     layer_two(5 * SECOND, steps - 5 * SECOND)
+    pl.when(has_earlier)(halo[0].wait_recv)
+    layer_one(0, SECOND)
     pl.when(has_earlier)(halo[1].wait_recv)
     layer_two(0, SECOND)
     far_one_head[...] = far_one[pl.ds(0, SECOND)].astype(jnp.bfloat16)
@@ -544,8 +536,9 @@
     back_one(0, SECOND)
     far_zero_head[...] = far_zero[pl.ds(0, FIRST)].astype(jnp.bfloat16)
     pl.when(has_earlier)(halo[3].start)
+    back_one(SECOND, steps // 2 - SECOND)
     scatter(0)
-    back_one(SECOND, steps - 2 * SECOND)
+    back_one(steps // 2, steps // 2 - SECOND)
     pl.when(has_later)(halo[2].wait_recv)
     back_one(steps - SECOND, SECOND)
     start(1)
@@ -568,8 +561,8 @@
 
     back_zero(0, steps - SECOND)
     pl.when(has_later)(halo[3].wait_recv)
+    back_zero(steps - SECOND, SECOND)
     scatter(1)
-    back_zero(steps - SECOND, SECOND)
 
     def column(k):
         return jnp.sum(acc[k], axis=0, keepdims=True)
@@ -606,8 +599,8 @@
 
     each(0, chunks, resolve)
     gather(1)
+    gather(2)
     share(0)
-    gather(2)
     share(1)
     share(2)
 
@@ -723,9 +716,9 @@
             *wide_blocks(PARTS),
             pltpu.VMEM((128, 128), f32),
             pltpu.VMEM((10, 8, 128), f32),
+            pltpu.VMEM((steps // ROWS, 2, 128), f32),
             pltpu.VMEM((2, 128), f32),
-            pltpu.VMEM((Z, 2, 128), f32),
-            pltpu.VMEM((X, 2, 128), f32),
+            pltpu.VMEM((TM, 2, 128), f32),
             pltpu.VMEM((4, 128), f32),
             pltpu.VMEM((Z, 4, 128), f32),
             pltpu.VMEM((X, 4, 128), f32),

time: 57.2 us -> 53.7 us (0.939)
  Pallas kernels: 56.3 us -> 52.8 us
    pallas_call x1, Pallas kernels: 54 us -> 50.5 us  [on_device(): pl.pallas_call(block_kernel, name='block', out_shape=(pltpu.VMEM((steps,...]
where the time goes in v6:
time: 53.7 us; the launch traced here: 53.6 us
  Pallas kernels  52.8 us (98%)
  between operations  0.81 us (2%)
    pallas_call x1, Pallas kernels, on_device(): pl.pallas_call(block_kernel, name='block', out_shape=(pltpu.VMEM((steps,...  50.5 us
    pallas_call x1, Pallas kernels, on_device(): pl.pallas_call(unpack_kernel, name='unpack', out_shape=(shape((steps, 128...  2.3 us

profile of v6, /device:TPU:1, one launch (start us, length us, event | category | flops | bytes accessed | tf_op | source)
XLA Modules:
  0.0 53.6 jit_solution(9121692491967592738)
XLA Ops:
  0.6 50.5 %block.1 = (f32[4096,128]{1,0:T(8,128)S(1)}, bf16[1024,128]{1,0:T(8,128)(2,1)S(1)}, bf16[1024,128]{1,0:T(8,128)(2,1)S(1)}, f32[256,128]{1,0:T(8,128)S(1)}) custom-call(f32[4096,128]{1,0:T(8,128)} %bitcast.9, f32[4096,128]{1,0:T(8,128)} %bitcast.10, bf16[128,128]{1,0:T(8,128)(2,1)} %w_in_hbm.1, bf16[2,256,256]{2,1,0:T(8,128)(2,1)} %bitcast.11, ...), custom_call_target="tpu_custom_call" | custom-call | tf_op jit(solution)/shard_map/block/pallas_call | solution.py:682
  51.1 2.3 %unpack.1 = (f32[4096,128]{1,0:T(8,128)}, f32[2,2,128,256]{3,2,1,0:T(8,128)}, f32[2,256]{1,0:T(2,128)}, f32[128,128]{1,0:T(8,128)}, f32[2,128,256]{2,1,0:T(8,128...) custom-call(f32[4096,128]{1,0:T(8,128)S(1)} %get-tuple-element.22.hat, ...), custom_call_target="tpu_custom_call" | custom-call | tf_op jit(solution)/shard_map/unpack/pallas_call | solution.py:754

commit v7 on v6

--- a/solution.py
+++ b/solution.py
@@ -536,9 +536,8 @@
     back_one(0, SECOND)
     far_zero_head[...] = far_zero[pl.ds(0, FIRST)].astype(jnp.bfloat16)
     pl.when(has_earlier)(halo[3].start)
-    back_one(SECOND, steps // 2 - SECOND)
+    back_one(SECOND, steps - 2 * SECOND)
     scatter(0)
-    back_one(steps // 2, steps // 2 - SECOND)
     pl.when(has_later)(halo[2].wait_recv)
     back_one(steps - SECOND, SECOND)
     start(1)

time: 53.7 us -> 53.5 us (level)
  no operation moved by 1% of the time
where the time goes in v7:
time: 53.5 us; the launch traced here: 53.4 us
  Pallas kernels  52.6 us (98%)
  between operations  0.81 us (2%)
    pallas_call x1, Pallas kernels, on_device(): pl.pallas_call(block_kernel, name='block', out_shape=(pltpu.VMEM((steps,...  50.3 us
    pallas_call x1, Pallas kernels, on_device(): pl.pallas_call(unpack_kernel, name='unpack', out_shape=(shape((steps, 128...  2.3 us

profile of v7, /device:TPU:1, one launch (start us, length us, event | category | flops | bytes accessed | tf_op | source)
XLA Modules:
  0.0 53.4 jit_solution(17083122251234523254)
XLA Ops:
  0.6 50.3 %block.1 = (f32[4096,128]{1,0:T(8,128)S(1)}, bf16[1024,128]{1,0:T(8,128)(2,1)S(1)}, bf16[1024,128]{1,0:T(8,128)(2,1)S(1)}, f32[256,128]{1,0:T(8,128)S(1)}) custom-call(f32[4096,128]{1,0:T(8,128)} %bitcast.9, f32[4096,128]{1,0:T(8,128)} %bitcast.10, bf16[128,128]{1,0:T(8,128)(2,1)} %w_in_hbm.1, bf16[2,256,256]{2,1,0:T(8,128)(2,1)} %bitcast.11, ...), custom_call_target="tpu_custom_call" | custom-call | tf_op jit(solution)/shard_map/block/pallas_call | solution.py:681
  50.9 2.3 %unpack.1 = (f32[4096,128]{1,0:T(8,128)}, f32[2,2,128,256]{3,2,1,0:T(8,128)}, f32[2,256]{1,0:T(2,128)}, f32[128,128]{1,0:T(8,128)}, f32[2,128,256]{2,1,0:T(8,128...) custom-call(f32[4096,128]{1,0:T(8,128)S(1)} %get-tuple-element.22.hat, ...), custom_call_target="tpu_custom_call" | custom-call | tf_op jit(solution)/shard_map/unpack/pallas_call | solution.py:753

commit v8 on v7

--- a/solution.py
+++ b/solution.py
@@ -383,14 +383,14 @@
         far_one[now] = carried[:, :128]
         near_one[now] = carried[:, 128:]
 
-    layer_two(5 * SECOND, steps - 5 * SECOND)
+    layer_two(4 * SECOND, steps - 4 * SECOND)
     pl.when(has_earlier)(halo[0].wait_recv)
     layer_one(0, SECOND)
     pl.when(has_earlier)(halo[1].wait_recv)
     layer_two(0, SECOND)
     far_one_head[...] = far_one[pl.ds(0, SECOND)].astype(jnp.bfloat16)
     pl.when(has_earlier)(halo[2].start)
-    layer_two(SECOND, 4 * SECOND)
+    layer_two(SECOND, 3 * SECOND)
 
     groups = (
         (early, early_pair, early_half, early_one, early_block, early_two, early_out, EARLY),

time: 53.5 us -> 53.1 us (level)
  no operation moved by 1% of the time
where the time goes in v8:
time: 53.1 us; the launch traced here: 53 us
  Pallas kernels  52.2 us (98%)
  between operations  0.81 us (2%)
    pallas_call x1, Pallas kernels, on_device(): pl.pallas_call(block_kernel, name='block', out_shape=(pltpu.VMEM((steps,...  49.9 us
    pallas_call x1, Pallas kernels, on_device(): pl.pallas_call(unpack_kernel, name='unpack', out_shape=(shape((steps, 128...  2.3 us

profile of v8, /device:TPU:1, one launch (start us, length us, event | category | flops | bytes accessed | tf_op | source)
XLA Modules:
  0.0 53.0 jit_solution(6614618285725036221)
XLA Ops:
  0.6 49.9 %block.1 = (f32[4096,128]{1,0:T(8,128)S(1)}, bf16[1024,128]{1,0:T(8,128)(2,1)S(1)}, bf16[1024,128]{1,0:T(8,128)(2,1)S(1)}, f32[256,128]{1,0:T(8,128)S(1)}) custom-call(f32[4096,128]{1,0:T(8,128)} %bitcast.9, f32[4096,128]{1,0:T(8,128)} %bitcast.10, bf16[128,128]{1,0:T(8,128)(2,1)} %w_in_hbm.1, bf16[2,256,256]{2,1,0:T(8,128)(2,1)} %bitcast.11, ...), custom_call_target="tpu_custom_call" | custom-call | tf_op jit(solution)/shard_map/block/pallas_call | solution.py:681
  50.5 2.3 %unpack.1 = (f32[4096,128]{1,0:T(8,128)}, f32[2,2,128,256]{3,2,1,0:T(8,128)}, f32[2,256]{1,0:T(2,128)}, f32[128,128]{1,0:T(8,128)}, f32[2,128,256]{2,1,0:T(8,128...) custom-call(f32[4096,128]{1,0:T(8,128)S(1)} %get-tuple-element.22.hat, ...), custom_call_target="tpu_custom_call" | custom-call | tf_op jit(solution)/shard_map/unpack/pallas_call | solution.py:753
